TPU v7x, 512 devices: a whole 4x4x16 slice. The times are simulated.
512 devices in a mesh: tm: 32 (over z, core), space: 16 (over x, y).
Axes of the slice: x: 4, y: 4, z: 16, core: 2. Of those that a mesh axis runs over, the one named last changes fastest.
Arguments:
- right_side: float32 [32, 128, 2048], P('tm', 'space'), may hold values from -160 to 160
- cell_terms: float32 [3, 128, 2048], P(None, 'space'), may hold values from -0.3 to 0.3, as said below
- polynomial: float32 [4], replicated, may hold values from -0.98 to 1.84, as said below
Outputs:
- solution: float32 [32, 128, 2048], P('tm', 'space')
- history: float32 [4], replicated
Inputs may be any that keep to these rules, and one draw needn't show every extreme that they name: `cell_terms`: component 0 lies in [0.06, 0.25]; components 1 and 2 in [-0.3, 0.3]. `polynomial`: each coefficient lies within 15 percent of 1.6, -0.85, 0.2, -0.018 in order.
All inputs are finite; a program needn't handle non-finite values.
Results may differ from a plain program's by a relative error of at most 0.0015.
Values sent between devices are 32-bit elements; how exact they have to be, the bound alone decides.
No kernel may reach another device: no remote copies, remote signals or barrier semaphores. Data moves between devices by JAX's collectives and lax.ppermute only.
A program may use at most 64 MiB of HBM per device.

v0:
```python
import jax
import jax.numpy as jnp
from jax import lax
from jax.sharding import PartitionSpec as P

KRYLOV = 4


def extended(block, sides, width):
    for axis, dim in sides:
        count = lax.axis_size(axis)
        forward = [(i, i + 1) for i in range(count - 1)]
        backward = [(target, source) for source, target in forward]
        low = lax.ppermute(
            lax.slice_in_dim(block, block.shape[dim] - width, None, axis=dim), axis, forward
        )
        high = lax.ppermute(lax.slice_in_dim(block, 0, width, axis=dim), axis, backward)
        block = jnp.concatenate([low, block, high], axis=dim)
    return block


def passed_along(value, axis, steps):
    count = lax.axis_size(axis)
    leading, last = (max(0, -steps), min(count, count - steps))
    return lax.ppermute(value, axis, [(source, source + steps) for source in range(leading, last)])


def stencil(padded, cell_terms):
    middle = padded[:, 1:-1]
    upper_row = padded[:, :-2]
    lower_row = padded[:, 2:]
    sideways = jnp.pad(middle, ((0, 0), (0, 0), (1, 1)))
    left_col = sideways[:, :, :-2]
    right_col = sideways[:, :, 2:]
    diffuse = cell_terms[0]
    drift_x = cell_terms[1]
    drift_y = cell_terms[2]
    return (
        (1.0 + 4.0 * diffuse) * middle
        - diffuse * (upper_row + lower_row + left_col + right_col)
        + 0.5 * drift_x * (right_col - left_col)
        + 0.5 * drift_y * (lower_row - upper_row)
    )


def rimmed(source):
    return extended(source, (("space", 1),), 1)


def horner_each(source, cell_terms, polynomial):
    running = polynomial[3] * source
    for degree in (2, 1, 0):
        running = polynomial[degree] * source + stencil(rimmed(running), cell_terms)
    return running


def apply_preconditioned(source, cell_terms, polynomial):
    lifted = horner_each(source, cell_terms, polynomial)
    carried = passed_along(lifted, "tm", 1)
    earlier = jnp.concatenate([carried, lifted[:-1]], axis=0)
    padded = rimmed(lifted)
    return (stencil(padded, cell_terms) - earlier, lifted)


def least_squares(columns, beta_norm):
    num_columns = len(columns)
    cosines = []
    sines = []
    target = [beta_norm] + [jnp.zeros_like(beta_norm) for position in range(num_columns)]
    history = []
    triangle = []
    for column_at in range(num_columns):
        column = list(columns[column_at])
        for earlier in range(column_at):
            first_entry = column[earlier]
            second_entry = column[earlier + 1]
            column[earlier] = cosines[earlier] * first_entry + sines[earlier] * second_entry
            column[earlier + 1] = cosines[earlier] * second_entry - sines[earlier] * first_entry
        radius = jnp.sqrt(
            column[column_at] * column[column_at] + column[column_at + 1] * column[column_at + 1]
        )
        cosine = column[column_at] / radius
        sine_part = column[column_at + 1] / radius
        column[column_at] = radius
        cosines.append(cosine)
        sines.append(sine_part)
        target[column_at + 1] = -sine_part * target[column_at]
        target[column_at] = cosine * target[column_at]
        history.append(jnp.abs(target[column_at + 1]))
        triangle.append(column[: column_at + 1])
    solved = [None for position in range(num_columns)]
    for row_at in reversed(range(num_columns)):
        running_sum = target[row_at]
        for later in range(row_at + 1, num_columns):
            running_sum = running_sum - triangle[later][row_at] * solved[later]
        solved[row_at] = running_sum / triangle[row_at][row_at]
    return (solved, history)


def body(right_side, cell_terms, polynomial):
    beta_norm = jnp.sqrt(lax.psum(jnp.sum(right_side * right_side), ("tm", "space")))
    krylov_basis = [right_side / beta_norm]
    lifted_basis = []
    columns = []
    for krylov_at in range(KRYLOV):
        mapped, kept = apply_preconditioned(krylov_basis[krylov_at], cell_terms, polynomial)
        lifted_basis.append(kept)
        remainder = mapped
        projections = []
        for vector in krylov_basis:
            weight = lax.psum(jnp.sum(remainder * vector), ("tm", "space"))
            remainder = remainder - weight * vector
            projections.append(weight)
        length = jnp.sqrt(lax.psum(jnp.sum(remainder * remainder), ("tm", "space")) + 1e-06)
        columns.append(projections + [length])
        krylov_basis.append(remainder / length)
    solved, history = least_squares(columns, beta_norm)
    solution = solved[0] * lifted_basis[0]
    for position in range(1, KRYLOV):
        solution = solution + solved[position] * lifted_basis[position]
    return (solution, jnp.stack(history))


def solution(mesh):
    in_specs = (P("tm", "space", None), P(None, "space", None), P())
    out_specs = (P("tm", "space", None), P())
    return jax.shard_map(body, mesh=mesh, in_specs=in_specs, out_specs=out_specs, check_vma=False)
```

profile of v0, /device:TPU:1, one launch (start us, length us, event | category | flops | bytes accessed | tf_op | source)
XLA Modules:
  0.0 1732.3 jit_solution(6418117610687830319)
XLA Ops:
  2.1 111.0 %psum.105 = f32[]{:T(128)} all-reduce(f32[]{:T(128)} %multiply_reduce_fusion.14), channel_id=1, replica_groups=mesh['tm'=32,'space'=16] {'tm','space'}, use_global_device_ids=true, to_apply=%region_1.0 | all-reduce | flops 1 | bytes 8 | tf_op jit(solution)/shard_map/psum | solution.py:101
  119.5 3.1 collective-permute-done.1
  124.2 3.4 collective-permute-start.2
  128.9 3.1 collective-permute-done.3
  132.7 4.3 collective-permute-start.4
  138.4 3.1 collective-permute-done.5
  142.2 7.2 collective-permute-start.8
  149.4 3.7 collective-permute-start.6
  154.5 3.4 collective-permute-done.7
  158.6 103.7 %psum.106 = f32[]{:T(128)} all-reduce(f32[]{:T(128)} %get-tuple-element.18), channel_id=1, replica_groups=mesh['tm'=32,'space'=16] {'tm','space'}, use_global_device_ids=true, to_apply=%region_3.4 | all-reduce | flops 1 | bytes 8 | tf_op jit(solution)/shard_map/psum | solution.py:111
  263.7 98.8 %psum.107 = f32[]{:T(128)} all-reduce(f32[]{:T(128)} %multiply_reduce_fusion.12), channel_id=1, replica_groups=mesh['tm'=32,'space'=16] {'tm','space'}, use_global_device_ids=true, to_apply=%region_5.6 | all-reduce | flops 1 | bytes 8 | tf_op jit(solution)/shard_map/psum | solution.py:114
  365.8 4.0 collective-permute-start.9
  371.2 3.6 collective-permute-start.11
  376.2 3.1 collective-permute-done.12
  380.0 3.5 collective-permute-start.13
  384.9 5.5 collective-permute-done.14
  391.1 8.0 collective-permute-start.17
  399.1 5.7 collective-permute-start.15
  406.2 3.4 collective-permute-done.16
  410.3 101.5 %psum.108 = f32[]{:T(128)} all-reduce(f32[]{:T(128)} %get-tuple-element.14), channel_id=1, replica_groups=mesh['tm'=32,'space'=16] {'tm','space'}, use_global_device_ids=true, to_apply=%region_7.8 | all-reduce | flops 1 | bytes 8 | tf_op jit(solution)/shard_map/psum | solution.py:111
  513.1 100.4 %psum.109 = f32[]{:T(128)} all-reduce(f32[]{:T(128)} %multiply_reduce_fusion.10), channel_id=1, replica_groups=mesh['tm'=32,'space'=16] {'tm','space'}, use_global_device_ids=true, to_apply=%region_9.10 | all-reduce | flops 1 | bytes 8 | tf_op jit(solution)/shard_map/psum | solution.py:111
  615.5 99.4 %psum.110 = f32[]{:T(128)} all-reduce(f32[]{:T(128)} %get-tuple-element.12), channel_id=1, replica_groups=mesh['tm'=32,'space'=16] {'tm','space'}, use_global_device_ids=true, to_apply=%region_11.12 | all-reduce | flops 1 | bytes 8 | tf_op jit(solution)/shard_map/psum | solution.py:114
  716.2 3.1 collective-permute-start.18
  720.6 3.1 collective-permute-done.19
  724.4 2.4 collective-permute-start.20
  728.1 3.1 collective-permute-done.21
  732.0 5.2 collective-permute-start.22
  738.5 3.1 collective-permute-done.23
  742.4 8.2 collective-permute-start.26
  750.6 3.7 collective-permute-start.24
  755.7 3.4 collective-permute-done.25
  759.8 101.5 %psum.111 = f32[]{:T(128)} all-reduce(f32[]{:T(128)} %get-tuple-element.10), channel_id=1, replica_groups=mesh['tm'=32,'space'=16] {'tm','space'}, use_global_device_ids=true, to_apply=%region_13.14 | all-reduce | flops 1 | bytes 8 | tf_op jit(solution)/shard_map/psum | solution.py:111
  862.5 100.3 %psum.112 = f32[]{:T(128)} all-reduce(f32[]{:T(128)} %multiply_reduce_fusion.7), channel_id=1, replica_groups=mesh['tm'=32,'space'=16] {'tm','space'}, use_global_device_ids=true, to_apply=%region_15.16 | all-reduce | flops 1 | bytes 8 | tf_op jit(solution)/shard_map/psum | solution.py:111
  964.6 99.4 %psum.113 = f32[]{:T(128)} all-reduce(f32[]{:T(128)} %get-tuple-element.8), channel_id=1, replica_groups=mesh['tm'=32,'space'=16] {'tm','space'}, use_global_device_ids=true, to_apply=%region_17.18 | all-reduce | flops 1 | bytes 8 | tf_op jit(solution)/shard_map/psum | solution.py:111
  1065.3 100.2 %psum.114 = f32[]{:T(128)} all-reduce(f32[]{:T(128)} %multiply_reduce_fusion.5), channel_id=1, replica_groups=mesh['tm'=32,'space'=16] {'tm','space'}, use_global_device_ids=true, to_apply=%region_19.20 | all-reduce | flops 1 | bytes 8 | tf_op jit(solution)/shard_map/psum | solution.py:114
  1167.4 3.0 collective-permute-start.27
  1171.7 3.1 collective-permute-done.28
  1175.5 2.5 collective-permute-start.29
  1179.5 3.1 collective-permute-done.30
  1183.4 5.2 collective-permute-start.31
  1189.9 3.1 collective-permute-done.32
  1193.7 7.4 collective-permute-start.35
  1201.2 3.7 collective-permute-start.33
  1215.5 103.5 %psum.115 = f32[]{:T(128)} all-reduce(f32[]{:T(128)} %get-tuple-element.4), channel_id=1, replica_groups=mesh['tm'=32,'space'=16] {'tm','space'}, use_global_device_ids=true, to_apply=%region_21.22 | all-reduce | flops 1 | bytes 8 | tf_op jit(solution)/shard_map/psum | solution.py:111
  1320.9 99.6 %psum.116 = f32[]{:T(128)} all-reduce(f32[]{:T(128)} %multiply_reduce_fusion.3), channel_id=1, replica_groups=mesh['tm'=32,'space'=16] {'tm','space'}, use_global_device_ids=true, to_apply=%region_23.24 | all-reduce | flops 1 | bytes 8 | tf_op jit(solution)/shard_map/psum | solution.py:111
  1423.1 100.3 %psum.117 = f32[]{:T(128)} all-reduce(f32[]{:T(128)} %get-tuple-element.2), channel_id=1, replica_groups=mesh['tm'=32,'space'=16] {'tm','space'}, use_global_device_ids=true, to_apply=%region_25.26 | all-reduce | flops 1 | bytes 8 | tf_op jit(solution)/shard_map/psum | solution.py:111
  1525.3 99.6 %psum.118 = f32[]{:T(128)} all-reduce(f32[]{:T(128)} %multiply_reduce_fusion.1), channel_id=1, replica_groups=mesh['tm'=32,'space'=16] {'tm','space'}, use_global_device_ids=true, to_apply=%region_27.28 | all-reduce | flops 1 | bytes 8 | tf_op jit(solution)/shard_map/psum | solution.py:111
  1628.7 100.1 %psum.119 = f32[]{:T(128)} all-reduce(f32[]{:T(128)} %multiply_reduce_fusion), channel_id=1, replica_groups=mesh['tm'=32,'space'=16] {'tm','space'}, use_global_device_ids=true, to_apply=%region_29.30 | all-reduce | flops 1 | bytes 8 | tf_op jit(solution)/shard_map/psum | solution.py:114
  (93 shorter events, 60.1 us)
Async XLA Ops:
  0.6 122.0 %copy-start = (f32[3,8,2048]{2,1,0:T(8,128)S(1)}, f32[3,8,2048]{2,1,0:T(8,128)}, u32[]{:S(2)}) copy-start(f32[3,8,2048]{2,1,0:T(8,128)} %param.4) | copy-start | bytes 589828
  116.9 2.6 collective-permute-start
  118.2 4.4 collective-permute-start.1
  122.6 9.3 copy-start.1
  124.2 4.7 collective-permute-start.2
  127.5 4.4 collective-permute-start.3
  132.7 5.6 collective-permute-start.4
  137.1 4.4 collective-permute-start.5
  142.2 15.6 collective-permute-start.8
  149.4 5.1 collective-permute-start.6
  153.2 4.7 collective-permute-start.7
  364.5 5.3 collective-permute-start.10
  365.8 4.8 collective-permute-start.9
  371.2 4.9 collective-permute-start.11
  374.9 4.4 collective-permute-start.12
  380.0 4.8 collective-permute-start.13
  383.6 6.8 collective-permute-start.14
  391.1 18.5 %collective-permute-start.17 = (f32[1,8,2048]{2,1,0:T(8,128)S(1)}, f32[1,8,2048]{2,1,0:T(8,128)S(1)}, u32[]{:S(2)}, u32[]{:S(2)}) collective-permute-start(f32[1,8,2048]{2,1,0:T(8,128)S(1)} %add_add_fusion.6), channel_id=1, source_target_pairs={{0,16},{16,32},{32,48},{48,64},{64,80},{80,96},{96,112},{112,128},... | collective-permute-start | bytes 196616 | tf_op jit(solution)/shard_map/ppermute | solution.py:25
  399.1 7.1 collective-permute-start.15
  404.8 4.7 collective-permute-start.16
  716.2 4.4 collective-permute-start.18
  719.3 4.4 collective-permute-start.19
  724.4 3.7 collective-permute-start.20
  726.8 4.4 collective-permute-start.21
  732.0 6.6 collective-permute-start.22
  737.2 4.4 collective-permute-start.23
  742.4 16.7 collective-permute-start.26
  750.6 5.1 collective-permute-start.24
  754.4 4.7 collective-permute-start.25
  1167.4 4.3 collective-permute-start.27
  1170.4 4.4 collective-permute-start.28
  1175.5 4.0 collective-permute-start.29
  1178.0 4.6 collective-permute-start.30
  1183.4 6.5 collective-permute-start.31
  1188.6 4.4 collective-permute-start.32
  1193.7 21.0 %collective-permute-start.35 = (f32[1,8,2048]{2,1,0:T(8,128)S(1)}, f32[1,8,2048]{2,1,0:T(8,128)S(1)}, u32[]{:S(2)}, u32[]{:S(2)}) collective-permute-start(f32[1,8,2048]{2,1,0:T(8,128)S(1)} %add_add_fusion), channel_id=1, source_target_pairs={{0,16},{16,32},{32,48},{48,64},{64,80},{80,96},{96,112},{112,128},... | collective-permute-start | bytes 196616 | tf_op jit(solution)/shard_map/ppermute | solution.py:25
  1201.2 13.5 collective-permute-start.33
  1205.0 9.8 collective-permute-start.34
where the time goes:
time: 1740 us; the launch traced here: 1730 us
  blocking collectives  1520 us (87%)
  starting transfers between devices  110 us (6%)
  waiting for transfers between devices  47.3 us (3%)
  other arithmetic  35.4 us (2%)
  between operations  18.6 us (1%)
    psum x10, blocking collectives, body(): weight = lax.psum(jnp.sum(remainder * vector), ('tm', 'space'))  1010 us
    psum x4, blocking collectives, body(): lax.psum(jnp.sum(remainder * remainder), ('tm', 'space')) + 1e-06  398 us
    psum x1, blocking collectives, body(): lax.psum(jnp.sum(right_side * right_side), ('tm', 'space'))  111 us
    ppermute x16, starting transfers between devices, extended(): lax.ppermute(lax.slice_in_dim(block, block.shape[dim] - width, None, axis...  58.5 us
    ppermute x16, waiting for transfers between devices, extended(): lax.ppermute(lax.slice_in_dim(block, 0, width, axis=dim), axis, backward)  46.4 us
  transfers between devices with their start and end apart: 36, of which 15 were waited for; matrix products, arithmetic and copies ran while one was open for 0% of the time, Pallas kernels for 0%

commit v1 on v0

v1 whole, which is shorter than its diff:
```python
import functools

import jax
import jax.numpy as jnp
from jax import lax
from jax.experimental import pallas as pl
from jax.experimental.pallas import tpu as pltpu
from jax.sharding import Mesh, PartitionSpec as P

KRYLOV = 4
OWN = 64
HALO = 32
LANES = 128
ROWS = 8
PAD = 8
CHUNK = 32
PAIRS = [(i, j) for i in range(KRYLOV + 1) for j in range(i, KRYLOV + 1)]
VMEM = pl.BlockSpec(memory_space=pltpu.VMEM)
SMEM = pl.BlockSpec(memory_space=pltpu.SMEM)
PARAMS = pltpu.CompilerParams(vmem_limit_bytes=40 * 1024 * 1024)


def windows(blocks, lane):
    zero = jnp.zeros_like(blocks[0])
    even = [zero] + [pltpu.roll(b, HALO, 1) for b in blocks]
    odd = [pltpu.roll(b, LANES - HALO, 1) for b in blocks] + [zero]
    out = []
    for k in range(len(blocks)):
        out.append(jnp.where(lane < HALO, even[k], even[k + 1]))
        out.append(jnp.where(lane < LANES - HALO, odd[k], odd[k + 1]))
    return out


def pack_kernel(now, before, earlier, terms, out):
    core = lax.axis_index("c")
    lane = lax.broadcasted_iota(jnp.int32, (ROWS, LANES), 1)
    tiles = now.shape[2] // LANES
    sources = [
        lambda cols: now[0, :, cols],
        lambda cols: before[0, :, cols],
        lambda cols: earlier[0, :, cols],
        lambda cols: terms[2 * core, :, cols],
        lambda cols: terms[1 + core, :, cols],
    ]
    for plane, source in enumerate(sources):
        blocks = [source(slice(k * LANES, (k + 1) * LANES)) for k in range(tiles)]
        for peer, window in enumerate(windows(blocks, lane)):
            out[peer, plane] = window


def krylov_kernel(strips, polynomial, got, out, coef, k0, k1, k2, k3, k4, z1, z2, z3, z4, work_x, work_y):
    rows = ROWS * strips
    times = KRYLOV + 2
    krylov = [k0, k1, k2, k3, k4]
    lifted = [z1, z2, z3, z4]
    lane = lax.broadcasted_iota(jnp.int32, (ROWS, LANES), 1)
    sub = lax.broadcasted_iota(jnp.int32, (ROWS, LANES), 0)
    block = lax.axis_index("c") * strips + lax.axis_index("s")
    first_col = (block == 0) & (lane == HALO)
    last_col = (block == 2 * strips - 1) & (lane == HALO + OWN - 1)

    edge = jnp.zeros((PAD, LANES), jnp.float32)
    for ref in krylov + lifted + [work_x, work_y]:
        for t in range(ref.shape[0]):
            ref[t, 0:PAD] = edge
            ref[t, PAD + rows :] = edge

    for s in range(strips):
        there = slice(s * ROWS, (s + 1) * ROWS)
        inner = slice(PAD + s * ROWS, PAD + (s + 1) * ROWS)
        for c in range(2):
            for plane in range(3):
                k0[times - 2 + c - 2 * plane, inner] = got[c * strips + s, plane]
        diffuse = got[s, 3]
        half_x = 0.5 * got[s, 4]
        half_y = 0.5 * got[strips + s, 3]
        north = -diffuse - half_y
        south = half_y - diffuse
        if s == 0:
            north = jnp.where(sub == 0, 0.0, north)
        if s == strips - 1:
            south = jnp.where(sub == ROWS - 1, 0.0, south)
        coef[0, there] = 1.0 + 4.0 * diffuse
        coef[1, there] = north
        coef[2, there] = south
        coef[3, there] = jnp.where(first_col, 0.0, -diffuse - half_x)
        coef[4, there] = jnp.where(last_col, 0.0, half_x - diffuse)

    def sweep(count, apply):
        def step(index, carry):
            at = pl.multiple_of(index * CHUNK, CHUNK)
            parts = [coef[i, pl.ds(at, CHUNK)] for i in range(5)]

            def stencil(ref, t):
                middle = ref[t, pl.ds(at + PAD, CHUNK)]
                north = ref[t, pl.ds(at + PAD - 1, CHUNK)]
                south = ref[t, pl.ds(at + PAD + 1, CHUNK)]
                west = pltpu.roll(middle, 1, 1)
                east = pltpu.roll(middle, LANES - 1, 1)
                value = (
                    (parts[0] * middle + parts[3] * west)
                    + (parts[1] * north + parts[2] * south)
                    + parts[4] * east
                )
                return value, middle

            for t in range(count):
                apply(t, pl.ds(at + PAD, CHUNK), stencil)
            return carry

        lax.fori_loop(0, rows // CHUNK, step, 0)

    for j in range(KRYLOV):
        source, target, upper = krylov[j], krylov[j + 1], lifted[j]
        count = times - j

        def first(t, at, stencil):
            value, middle = stencil(source, t)
            work_x[t, at] = polynomial[2] * middle + polynomial[3] * value

        def second(t, at, stencil):
            value, _ = stencil(work_x, t)
            work_y[t, at] = polynomial[1] * source[t, at] + value

        def third(t, at, stencil):
            value, _ = stencil(work_y, t)
            upper[t, at] = polynomial[0] * source[t, at] + value

        def fourth(t, at, stencil):
            value, _ = stencil(upper, t + 1)
            target[t, at] = value - upper[t, at] - source[t + 1, at]

        sweep(count, first)
        sweep(count, second)
        sweep(count, third)
        sweep(count - 1, fourth)

    sums = [jnp.zeros((ROWS, LANES), jnp.float32) for _ in PAIRS]

    def gram(index, sums):
        at = pl.ds(pl.multiple_of(index * ROWS, ROWS) + PAD, ROWS)
        sums = list(sums)
        for own in range(2):
            vectors = [ref[ref.shape[0] - 2 + own, at] for ref in krylov]
            for n, (i, j) in enumerate(PAIRS):
                sums[n] = sums[n] + vectors[i] * vectors[j]
        return tuple(sums)

    sums = lax.fori_loop(0, strips, gram, tuple(sums))
    row = lax.broadcasted_iota(jnp.int32, (ROWS, LANES), 0)
    mine = (lane >= HALO) & (lane < HALO + OWN)
    packed = jnp.zeros((1, LANES), jnp.float32)
    for n, total in enumerate(sums):
        value = jnp.sum(jnp.where(mine, total, 0.0), axis=0, keepdims=True)
        value = jnp.sum(value, axis=1, keepdims=True)
        packed = packed + jnp.where(lane[0:1] == n, value, 0.0)
    packed = jnp.where(row == 0, packed, 0.0)

    for c in range(2):
        for s in range(strips):
            peer = c * strips + s
            at = slice(PAD + s * ROWS, PAD + (s + 1) * ROWS)
            for pair in range(2):
                low = lifted[2 * pair]
                high = lifted[2 * pair + 1]
                left = pltpu.roll(low[low.shape[0] - 2 + c, at], LANES - HALO, 1)
                right = pltpu.roll(high[high.shape[0] - 2 + c, at], HALO, 1)
                out[peer, pair] = jnp.where(lane < OWN, left, right)
            out[peer, 2] = packed


def least_squares(columns, beta_norm):
    num_columns = len(columns)
    cosines = []
    sines = []
    target = [beta_norm] + [jnp.zeros_like(beta_norm) for position in range(num_columns)]
    history = []
    triangle = []
    for column_at in range(num_columns):
        column = list(columns[column_at])
        for earlier in range(column_at):
            first_entry = column[earlier]
            second_entry = column[earlier + 1]
            column[earlier] = cosines[earlier] * first_entry + sines[earlier] * second_entry
            column[earlier + 1] = cosines[earlier] * second_entry - sines[earlier] * first_entry
        radius = jnp.sqrt(
            column[column_at] * column[column_at] + column[column_at + 1] * column[column_at + 1]
        )
        cosine = column[column_at] / radius
        sine_part = column[column_at + 1] / radius
        column[column_at] = radius
        cosines.append(cosine)
        sines.append(sine_part)
        target[column_at + 1] = -sine_part * target[column_at]
        target[column_at] = cosine * target[column_at]
        history.append(jnp.abs(target[column_at + 1]))
        triangle.append(column[: column_at + 1])
    solved = [None for position in range(num_columns)]
    for row_at in reversed(range(num_columns)):
        running_sum = target[row_at]
        for later in range(row_at + 1, num_columns):
            running_sum = running_sum - triangle[later][row_at] * solved[later]
        solved[row_at] = running_sum / triangle[row_at][row_at]
    return (solved, history)


def cycle(gram):
    def product(left, right):
        total = None
        for i, a in enumerate(left):
            for j, b in enumerate(right):
                term = a * b * gram[min(i, j), max(i, j)]
                total = term if total is None else total + term
        return total

    beta_norm = jnp.sqrt(gram[0, 0])
    basis = [[1.0 / beta_norm]]
    columns = []
    for at in range(KRYLOV):
        newest = basis[-1]
        image = list(newest) + [None]
        for m, value in enumerate(newest):
            image[m + 1] = value if image[m + 1] is None else image[m + 1] + value
        projections = [product(image, vector) for vector in basis]
        rest = list(image)
        for vector, weight in zip(basis, projections):
            for m, value in enumerate(vector):
                rest[m] = rest[m] - weight * value
        length = jnp.sqrt(jnp.maximum(product(rest, rest), 0.0) + 1e-06)
        columns.append(projections + [length])
        basis.append([value / length for value in rest])
    solved, history = least_squares(columns, beta_norm)
    weights = []
    for m in range(KRYLOV):
        total = None
        for j in range(m, KRYLOV):
            term = solved[j] * basis[j][m]
            total = term if total is None else total + term
        weights.append(total)
    return weights, history


def combine_kernel(partial, got, solution, history):
    lane = lax.broadcasted_iota(jnp.int32, (ROWS, LANES), 1)
    total = jnp.sum(partial[:, 0, :], axis=0, keepdims=True)
    gram = {}
    for n, pair in enumerate(PAIRS):
        gram[pair] = jnp.sum(jnp.where(lane[0:1] == n, total, 0.0), axis=1, keepdims=True)
    weights, norms = cycle(gram)
    for n, norm in enumerate(norms):
        history[n] = jnp.max(norm)
    low = jnp.where(lane < OWN, weights[0], weights[1])
    high = jnp.where(lane < OWN, weights[2], weights[3])

    def block(index):
        value = low * got[index, 0] + high * got[index, 1]
        return value + pltpu.roll(value, OWN, 1)

    for k in range(got.shape[0] // 2):
        solution[0, :, k * LANES : (k + 1) * LANES] = jnp.where(lane < OWN, block(2 * k), block(2 * k + 1))


def body(layers, strips, right_side, cell_terms, polynomial):
    f32 = jnp.float32
    peers = 2 * strips
    rows = ROWS * strips
    layer = ("c", "s")
    before = lax.ppermute(right_side, "z", [(i, i + 1) for i in range(layers - 1)])
    earlier = lax.ppermute(right_side, "z", [(i, i + 2) for i in range(layers - 2)])
    sent = pl.pallas_call(
        pack_kernel,
        out_shape=jax.ShapeDtypeStruct((peers, 5, ROWS, LANES), f32),
        in_specs=[VMEM] * 4,
        out_specs=VMEM,
        compiler_params=PARAMS,
        name="pack",
    )(right_side, before, earlier, cell_terms)
    got = lax.all_to_all(sent, layer, 0, 0, tiled=True)
    times = KRYLOV + 2
    field = lambda count: pltpu.VMEM((count, rows + 2 * PAD, LANES), f32)
    sent = pl.pallas_call(
        functools.partial(krylov_kernel, strips),
        out_shape=jax.ShapeDtypeStruct((peers, 3, ROWS, LANES), f32),
        in_specs=[SMEM, VMEM],
        out_specs=VMEM,
        scratch_shapes=[pltpu.VMEM((5, rows, LANES), f32)]
        + [field(times - j) for j in range(KRYLOV + 1)]
        + [field(times - j) for j in range(KRYLOV)]
        + [field(times), field(times)],
        compiler_params=PARAMS,
        name="krylov",
    )(polynomial, got)
    got = lax.all_to_all(sent, layer, 0, 0, tiled=True)
    partial = jnp.sum(got[:, 2, 0:1, :], axis=0)
    partial = jnp.broadcast_to(partial[None], (layers, 1, LANES))
    partial = lax.all_to_all(partial, "z", 0, 0, tiled=True)
    return pl.pallas_call(
        combine_kernel,
        out_shape=(jax.ShapeDtypeStruct(right_side.shape, f32), jax.ShapeDtypeStruct((KRYLOV,), f32)),
        in_specs=[VMEM, VMEM],
        out_specs=(VMEM, SMEM),
        compiler_params=PARAMS,
        name="combine",
    )(partial, got)


def solution(mesh):
    layers = mesh.shape["tm"] // 2
    strips = mesh.shape["space"]
    fine = Mesh(mesh.devices.reshape(layers, 2, strips), ("z", "c", "s"))
    in_specs = (P(("z", "c"), "s", None), P(None, "s", None), P())
    out_specs = (P(("z", "c"), "s", None), P())
    return jax.shard_map(
        functools.partial(body, layers, strips), mesh=fine, in_specs=in_specs, out_specs=out_specs, check_vma=False
    )
```

time: 1740 us -> 85.6 us (0.05)
  blocking collectives: 1520 us -> 62.5 us
  starting transfers between devices: 110 us -> 9.27 us
  waiting for transfers between devices: 47.3 us -> 1.62 us
  other arithmetic: 35.4 us -> 0.05 us
  between operations: 18.6 us -> 0.68 us
    psum x15 -> x0, blocking collectives: 1520 us -> none  [the longest x10 1010 us: body(): weight = lax.psum(jnp.sum(remainder * vector), ('tm', 'space'))]
    ppermute x36 -> x2, starting transfers between devices: 110 us -> 9.27 us  [the longest x1 4.9 us: body(): lax.ppermute(right_side, 'z', [(i, i + 2) for i in range(layers - 2)])]
    all_to_all x0 -> x3, blocking collectives: none -> 62.5 us  [the longest x2 35.2 us: body(): got = lax.all_to_all(sent, layer, 0, 0, tiled=True)]
    ppermute x36 -> x2, waiting for transfers between devices: 47.3 us -> 1.62 us  [the longest x1 1.62 us: body(): lax.ppermute(right_side, 'z', [(i, i + 2) for i in range(layers - 2)])]
    reduce_sum x15 -> x1, other arithmetic: 19.7 us -> 0.05 us  [body(): partial = jnp.sum(got[:, 2, 0:1, :], axis=0)]
  transfers between devices with their start and end apart: 36 -> 2, of which waited for: 15 -> 1; matrix products, arithmetic and copies ran while one was open for 0% -> 0% of each run, Pallas kernels for 0% -> 0%
where the time goes in v1:
time: 85.6 us; the launch traced here: 85.2 us
  blocking collectives  62.5 us (73%)
  Pallas kernels  9.3 us (11%)
  starting transfers between devices  9.27 us (11%)
  local copies, waits for them, and re-layouts  1.78 us (2%)
  waiting for transfers between devices  1.62 us (2%)
    all_to_all x2, blocking collectives, body(): got = lax.all_to_all(sent, layer, 0, 0, tiled=True)  35.2 us
    all_to_all x1, blocking collectives, body(): partial = lax.all_to_all(partial, 'z', 0, 0, tiled=True)  27.3 us
    pallas_call x1, Pallas kernels, body(): pl.pallas_call(functools.partial(krylov_kernel, strips), out_shape=jax.Sh...  7.97 us
    ppermute x1, starting transfers between devices, body(): lax.ppermute(right_side, 'z', [(i, i + 2) for i in range(layers - 2)])  4.9 us
    ppermute x1, starting transfers between devices, body(): lax.ppermute(right_side, 'z', [(i, i + 1) for i in range(layers - 1)])  4.37 us
    unnamed x6, local copies, waits for them, and re-layouts  1.77 us
  transfers between devices with their start and end apart: 2, of which 1 were waited for; matrix products, arithmetic and copies ran while one was open for 0% of the time, Pallas kernels for 0%

profile of v1, /device:TPU:1, one launch (start us, length us, event | category | flops | bytes accessed | tf_op | source)
XLA Modules:
  0.0 85.2 jit_solution(1772751531321650257)
XLA Ops:
  0.6 4.4 %collective-permute-start = (f32[1,8,2048]{2,1,0:T(8,128)}, f32[1,8,2048]{2,1,0:T(8,128)S(1)}, u32[]{:S(2)}, u32[]{:S(2)}) collective-permute-start(f32[1,8,2048]{2,1,0:T(8,128)} %now.1), channel_id=1, source_target_pairs={{0,32},{32,64},{64,96},{96,128},{128,160},{160,192},{192,224},{224... | collective-permute-start | bytes 196616 | tf_op jit(solution)/shard_map/ppermute | solution.py:268
  5.0 4.9 %collective-permute-start.1 = (f32[1,8,2048]{2,1,0:T(8,128)}, f32[1,8,2048]{2,1,0:T(8,128)S(1)}, u32[]{:S(2)}, u32[]{:S(2)}) collective-permute-start(f32[1,8,2048]{2,1,0:T(8,128)} %now.1), channel_id=1, source_target_pairs={{0,64},{32,96},{64,128},{96,160},{128,192},{160,224},{192,256},{22... | collective-permute-start | bytes 196616 | tf_op jit(solution)/shard_map/ppermute | solution.py:269
  9.9 0.0 collective-permute-done.before
  9.9 1.6 %collective-permute-done.1.earlier = f32[1,8,2048]{2,1,0:T(8,128)S(1)} collective-permute-done((f32[1,8,2048]{2,1,0:T(8,128)}, f32[1,8,2048]{2,1,0:T(8,128)S(1)}, u32[]{:S(2)}, u32[]{:S(2)}) %collective-permute-start.1) | collective-permute-done | bytes 65568 | tf_op jit(solution)/shard_map/ppermute | solution.py:269
  11.5 0.0 copy-start
  11.5 0.9 %copy-done = f32[3,8,2048]{2,1,0:T(8,128)S(1)} copy-done((f32[3,8,2048]{2,1,0:T(8,128)S(1)}, f32[3,8,2048]{2,1,0:T(8,128)}, u32[]{:S(2)}) %copy-start) | copy-done | bytes 196632
  12.5 0.0 copy-start.1
  12.5 0.8 copy-done.1
  13.3 0.2 pack.1
  13.5 0.0 copy-start.2
  13.6 21.2 %all_to_all.15.got = f32[32,5,8,128]{3,2,1,0:T(8,128)S(1)} all-to-all(f32[32,5,8,128]{3,2,1,0:T(8,128)S(1)} %pack.1), channel_id=1, replica_groups=mesh['z'=16,'c'=2,'s'=16] {'c','s'}, dimensions={0} | all-to-all | bytes 1310720 | tf_op jit(solution)/shard_map/all_to_all | solution.py:278
  34.8 0.0 copy-done.2
  34.8 8.0 %krylov.1 = f32[32,3,8,128]{3,2,1,0:T(8,128)S(1)} custom-call(f32[4]{0:T(128)S(1)} %copy-done.2, f32[32,5,8,128]{3,2,1,0:T(8,128)S(1)} %all_to_all.15.got), custom_call_target="tpu_custom_call" | custom-call | tf_op jit(solution)/shard_map/krylov/pallas_call | solution.py:281
  42.7 14.0 %all_to_all.16.got = f32[32,3,8,128]{3,2,1,0:T(8,128)S(1)} all-to-all(f32[32,3,8,128]{3,2,1,0:T(8,128)S(1)} %krylov.1), channel_id=1, replica_groups=mesh['z'=16,'c'=2,'s'=16] {'c','s'}, dimensions={0} | all-to-all | bytes 786432 | tf_op jit(solution)/shard_map/all_to_all | solution.py:293
  56.8 27.3 %all_to_all.17.partial = f32[16,1,128]{2,1,0:T(1,128)S(1)} all-to-all(f32[16,1,128]{2,1,0:T(1,128)S(1)} %broadcast_in_dim.2), channel_id=1, replica_groups=mesh['z'=16,'c'=2,'s'=16] {'z'}, dimensions={0} | all-to-all | bytes 16384 | tf_op jit(solution)/shard_map/all_to_all | solution.py:296
  84.1 1.1 %combine.1 = (f32[1,8,2048]{2,1,0:T(8,128)}, f32[4]{0:T(128)}) custom-call(f32[16,1,128]{2,1,0:T(1,128)S(1)} %all_to_all.17.partial, f32[32,3,8,128]{3,2,1,0:T(8,128)S(1)} %all_to_all.16.got), custom_call_target="tpu_custom_call" | custom-call | tf_op jit(solution)/shard_map/combine/pallas_call | solution.py:297
  (2 shorter events, 0.1 us)
Async XLA Ops:
  0.6 9.3 %collective-permute-start = (f32[1,8,2048]{2,1,0:T(8,128)}, f32[1,8,2048]{2,1,0:T(8,128)S(1)}, u32[]{:S(2)}, u32[]{:S(2)}) collective-permute-start(f32[1,8,2048]{2,1,0:T(8,128)} %now.1), channel_id=1, source_target_pairs={{0,32},{32,64},{64,96},{96,128},{128,160},{160,192},{192,224},{224... | collective-permute-start | bytes 196616 | tf_op jit(solution)/shard_map/ppermute | solution.py:268
  5.0 6.5 %collective-permute-start.1 = (f32[1,8,2048]{2,1,0:T(8,128)}, f32[1,8,2048]{2,1,0:T(8,128)S(1)}, u32[]{:S(2)}, u32[]{:S(2)}) collective-permute-start(f32[1,8,2048]{2,1,0:T(8,128)} %now.1), channel_id=1, source_target_pairs={{0,64},{32,96},{64,128},{96,160},{128,192},{160,224},{192,256},{22... | collective-permute-start | bytes 196616 | tf_op jit(solution)/shard_map/ppermute | solution.py:269
  11.5 0.9 %copy-start = (f32[3,8,2048]{2,1,0:T(8,128)S(1)}, f32[3,8,2048]{2,1,0:T(8,128)}, u32[]{:S(2)}) copy-start(f32[3,8,2048]{2,1,0:T(8,128)} %terms.1) | copy-start | bytes 589828
  12.5 0.8 copy-start.1
  13.5 21.2 %copy-start.2 = (f32[4]{0:T(128)S(1)}, f32[4]{0:T(128)}, u32[]{:S(2)}) copy-start(f32[4]{0:T(128)} %polynomial.1) | copy-start | bytes 52

commit v2 on v1

--- a/solution.py
+++ b/solution.py
@@ -13,7 +13,7 @@
 LANES = 128
 ROWS = 8
 PAD = 8
-CHUNK = 32
+CHUNK = 128
 PAIRS = [(i, j) for i in range(KRYLOV + 1) for j in range(i, KRYLOV + 1)]
 VMEM = pl.BlockSpec(memory_space=pltpu.VMEM)
 SMEM = pl.BlockSpec(memory_space=pltpu.SMEM)
@@ -31,21 +31,25 @@
     return out
 
 
-def pack_kernel(now, before, earlier, terms, out):
-    core = lax.axis_index("c")
+def spread(sources, out, plane):
     lane = lax.broadcasted_iota(jnp.int32, (ROWS, LANES), 1)
-    tiles = now.shape[2] // LANES
-    sources = [
-        lambda cols: now[0, :, cols],
-        lambda cols: before[0, :, cols],
-        lambda cols: earlier[0, :, cols],
-        lambda cols: terms[2 * core, :, cols],
-        lambda cols: terms[1 + core, :, cols],
-    ]
-    for plane, source in enumerate(sources):
-        blocks = [source(slice(k * LANES, (k + 1) * LANES)) for k in range(tiles)]
+    for source in sources:
+        blocks = [source[:, k * LANES : (k + 1) * LANES] for k in range(source.shape[1] // LANES)]
         for peer, window in enumerate(windows(blocks, lane)):
             out[peer, plane] = window
+        plane += 1
+
+
+def own_kernel(now, terms, out):
+    core = lax.axis_index("c")
+    spread([now.at[0], terms.at[2 * core], terms.at[1 + core]], out, 0)
+
+
+def pack_kernel(own, before, earlier, out):
+    for peer in range(out.shape[0]):
+        for plane in range(3):
+            out[peer, plane] = own[peer, plane]
+    spread([before.at[0], earlier.at[0]], out, 3)
 
 
 def krylov_kernel(strips, polynomial, got, out, coef, k0, k1, k2, k3, k4, z1, z2, z3, z4, work_x, work_y):
@@ -70,10 +74,10 @@
         inner = slice(PAD + s * ROWS, PAD + (s + 1) * ROWS)
         for c in range(2):
             for plane in range(3):
-                k0[times - 2 + c - 2 * plane, inner] = got[c * strips + s, plane]
-        diffuse = got[s, 3]
-        half_x = 0.5 * got[s, 4]
-        half_y = 0.5 * got[strips + s, 3]
+                k0[times - 2 + c - 2 * plane, inner] = got[c * strips + s, (0, 3, 4)[plane]]
+        diffuse = got[s, 1]
+        half_x = 0.5 * got[s, 2]
+        half_y = 0.5 * got[strips + s, 1]
         north = -diffuse - half_y
         south = half_y - diffuse
         if s == 0:
@@ -265,16 +269,25 @@
     peers = 2 * strips
     rows = ROWS * strips
     layer = ("c", "s")
+    earlier = lax.ppermute(right_side, "z", [(i, i + 2) for i in range(layers - 2)])
     before = lax.ppermute(right_side, "z", [(i, i + 1) for i in range(layers - 1)])
-    earlier = lax.ppermute(right_side, "z", [(i, i + 2) for i in range(layers - 2)])
+    own = pl.pallas_call(
+        own_kernel,
+        out_shape=jax.ShapeDtypeStruct((peers, 3, ROWS, LANES), f32),
+        in_specs=[VMEM] * 2,
+        out_specs=VMEM,
+        compiler_params=PARAMS,
+        cost_estimate=pl.CostEstimate(flops=1000000, bytes_accessed=4000000, transcendentals=0),
+        name="own",
+    )(right_side, cell_terms)
     sent = pl.pallas_call(
         pack_kernel,
         out_shape=jax.ShapeDtypeStruct((peers, 5, ROWS, LANES), f32),
-        in_specs=[VMEM] * 4,
+        in_specs=[VMEM] * 3,
         out_specs=VMEM,
         compiler_params=PARAMS,
         name="pack",
-    )(right_side, before, earlier, cell_terms)
+    )(own, before, earlier)
     got = lax.all_to_all(sent, layer, 0, 0, tiled=True)
     times = KRYLOV + 2
     field = lambda count: pltpu.VMEM((count, rows + 2 * PAD, LANES), f32)

time: 85.6 us -> 77.7 us (0.908)
  Pallas kernels: 9.3 us -> 4.94 us
  blocking collectives: 62.5 us -> 60.7 us
  waiting for transfers between devices: 1.62 us -> 0.01 us
    pallas_call x1, Pallas kernels: 7.97 us -> 3.55 us  [body(): pl.pallas_call(functools.partial(krylov_kernel, strips), out_shape=jax.Sh...]
    ppermute x1, waiting for transfers between devices: 1.62 us -> 0.01 us  [body(): lax.ppermute(right_side, 'z', [(i, i + 2) for i in range(layers - 2)])]
    all_to_all x1, blocking collectives: 27.3 us -> 25.8 us  [body(): partial = lax.all_to_all(partial, 'z', 0, 0, tiled=True)]
  transfers between devices with their start and end apart: 2 -> 2, of which waited for: 1 -> 0; matrix products, arithmetic and copies ran while one was open for 0% -> 0% of each run, Pallas kernels for 0% -> 0%
where the time goes in v2:
time: 77.7 us; the launch traced here: 77.4 us
  blocking collectives  60.7 us (78%)
  starting transfers between devices  9.27 us (12%)
  Pallas kernels  4.94 us (6%)
  local copies, waits for them, and re-layouts  1.77 us (2%)
    all_to_all x2, blocking collectives, body(): got = lax.all_to_all(sent, layer, 0, 0, tiled=True)  34.9 us
    all_to_all x1, blocking collectives, body(): partial = lax.all_to_all(partial, 'z', 0, 0, tiled=True)  25.8 us
    ppermute x1, starting transfers between devices, body(): lax.ppermute(right_side, 'z', [(i, i + 2) for i in range(layers - 2)])  5.73 us
    pallas_call x1, Pallas kernels, body(): pl.pallas_call(functools.partial(krylov_kernel, strips), out_shape=jax.Sh...  3.55 us
    ppermute x1, starting transfers between devices, body(): lax.ppermute(right_side, 'z', [(i, i + 1) for i in range(layers - 1)])  3.54 us
    unnamed x6, local copies, waits for them, and re-layouts  1.77 us
  transfers between devices with their start and end apart: 2, of which 0 were waited for; matrix products, arithmetic and copies ran while one was open for 0% of the time, Pallas kernels for 0%

profile of v2, /device:TPU:1, one launch (start us, length us, event | category | flops | bytes accessed | tf_op | source)
XLA Modules:
  0.0 77.4 jit_solution(6691960573998064192)
XLA Ops:
  0.6 5.7 %collective-permute-start.1 = (f32[1,8,2048]{2,1,0:T(8,128)}, f32[1,8,2048]{2,1,0:T(8,128)S(1)}, u32[]{:S(2)}, u32[]{:S(2)}) collective-permute-start(f32[1,8,2048]{2,1,0:T(8,128)} %now.1), channel_id=1, source_target_pairs={{0,64},{32,96},{64,128},{96,160},{128,192},{160,224},{192,256},{22... | collective-permute-start | bytes 196616 | tf_op jit(solution)/shard_map/ppermute | solution.py:272
  6.4 3.5 %collective-permute-start = (f32[1,8,2048]{2,1,0:T(8,128)}, f32[1,8,2048]{2,1,0:T(8,128)S(1)}, u32[]{:S(2)}, u32[]{:S(2)}) collective-permute-start(f32[1,8,2048]{2,1,0:T(8,128)} %now.1), channel_id=1, source_target_pairs={{0,32},{32,64},{64,96},{96,128},{128,160},{160,192},{192,224},{224... | collective-permute-start | bytes 196616 | tf_op jit(solution)/shard_map/ppermute | solution.py:273
  9.9 0.0 copy-start
  9.9 0.9 %copy-done = f32[3,8,2048]{2,1,0:T(8,128)S(1)} copy-done((f32[3,8,2048]{2,1,0:T(8,128)S(1)}, f32[3,8,2048]{2,1,0:T(8,128)}, u32[]{:S(2)}) %copy-start) | copy-done | bytes 196632
  10.8 0.0 copy-start.1
  10.8 0.8 %copy-done.1 = f32[1,8,2048]{2,1,0:T(8,128)S(1)} copy-done((f32[1,8,2048]{2,1,0:T(8,128)S(1)}, f32[1,8,2048]{2,1,0:T(8,128)}, u32[]{:S(2)}) %copy-start.1) | copy-done | bytes 65560
  11.7 0.2 own.1
  11.9 0.0 collective-permute-done.1.earlier
  11.9 0.0 collective-permute-done.before
  11.9 0.1 pack.1
  12.0 0.0 copy-start.2
  12.0 20.9 %all_to_all.15.got = f32[32,5,8,128]{3,2,1,0:T(8,128)S(1)} all-to-all(f32[32,5,8,128]{3,2,1,0:T(8,128)S(1)} %pack.1), channel_id=1, replica_groups=mesh['z'=16,'c'=2,'s'=16] {'c','s'}, dimensions={0} | all-to-all | bytes 1310720 | tf_op jit(solution)/shard_map/all_to_all | solution.py:291
  32.9 0.0 copy-done.2
  32.9 3.5 %krylov.1 = f32[32,3,8,128]{3,2,1,0:T(8,128)S(1)} custom-call(f32[4]{0:T(128)S(1)} %copy-done.2, f32[32,5,8,128]{3,2,1,0:T(8,128)S(1)} %all_to_all.15.got), custom_call_target="tpu_custom_call" | custom-call | tf_op jit(solution)/shard_map/krylov/pallas_call | solution.py:294
  36.5 14.0 %all_to_all.16.got = f32[32,3,8,128]{3,2,1,0:T(8,128)S(1)} all-to-all(f32[32,3,8,128]{3,2,1,0:T(8,128)S(1)} %krylov.1), channel_id=1, replica_groups=mesh['z'=16,'c'=2,'s'=16] {'c','s'}, dimensions={0} | all-to-all | bytes 786432 | tf_op jit(solution)/shard_map/all_to_all | solution.py:306
  50.5 25.8 %all_to_all.17.partial = f32[16,1,128]{2,1,0:T(1,128)S(1)} all-to-all(f32[16,1,128]{2,1,0:T(1,128)S(1)} %broadcast_in_dim.2), channel_id=1, replica_groups=mesh['z'=16,'c'=2,'s'=16] {'z'}, dimensions={0} | all-to-all | bytes 16384 | tf_op jit(solution)/shard_map/all_to_all | solution.py:309
  76.3 1.1 %combine.1 = (f32[1,8,2048]{2,1,0:T(8,128)}, f32[4]{0:T(128)}) custom-call(f32[16,1,128]{2,1,0:T(1,128)S(1)} %all_to_all.17.partial, f32[32,3,8,128]{3,2,1,0:T(8,128)S(1)} %all_to_all.16.got), custom_call_target="tpu_custom_call" | custom-call | tf_op jit(solution)/shard_map/combine/pallas_call | solution.py:310
  (2 shorter events, 0.1 us)
Async XLA Ops:
  0.6 11.2 %collective-permute-start.1 = (f32[1,8,2048]{2,1,0:T(8,128)}, f32[1,8,2048]{2,1,0:T(8,128)S(1)}, u32[]{:S(2)}, u32[]{:S(2)}) collective-permute-start(f32[1,8,2048]{2,1,0:T(8,128)} %now.1), channel_id=1, source_target_pairs={{0,64},{32,96},{64,128},{96,160},{128,192},{160,224},{192,256},{22... | collective-permute-start | bytes 196616 | tf_op jit(solution)/shard_map/ppermute | solution.py:272
  6.4 5.5 %collective-permute-start = (f32[1,8,2048]{2,1,0:T(8,128)}, f32[1,8,2048]{2,1,0:T(8,128)S(1)}, u32[]{:S(2)}, u32[]{:S(2)}) collective-permute-start(f32[1,8,2048]{2,1,0:T(8,128)} %now.1), channel_id=1, source_target_pairs={{0,32},{32,64},{64,96},{96,128},{128,160},{160,192},{192,224},{224... | collective-permute-start | bytes 196616 | tf_op jit(solution)/shard_map/ppermute | solution.py:273
  9.9 0.9 %copy-start = (f32[3,8,2048]{2,1,0:T(8,128)S(1)}, f32[3,8,2048]{2,1,0:T(8,128)}, u32[]{:S(2)}) copy-start(f32[3,8,2048]{2,1,0:T(8,128)} %terms.1) | copy-start | bytes 589828
  10.8 0.8 %copy-start.1 = (f32[1,8,2048]{2,1,0:T(8,128)S(1)}, f32[1,8,2048]{2,1,0:T(8,128)}, u32[]{:S(2)}) copy-start(f32[1,8,2048]{2,1,0:T(8,128)} %now.1) | copy-start | bytes 196612
  12.0 20.9 %copy-start.2 = (f32[4]{0:T(128)S(1)}, f32[4]{0:T(128)}, u32[]{:S(2)}) copy-start(f32[4]{0:T(128)} %polynomial.1) | copy-start | bytes 52

commit v3 on v2

--- a/solution.py
+++ b/solution.py
@@ -9,7 +9,9 @@
 
 KRYLOV = 4
 OWN = 64
-HALO = 32
+HALO = 16
+WIDE = OWN + 2 * HALO
+HALF = 4
 LANES = 128
 ROWS = 8
 PAD = 8
@@ -20,36 +22,61 @@
 PARAMS = pltpu.CompilerParams(vmem_limit_bytes=40 * 1024 * 1024)
 
 
-def windows(blocks, lane):
-    zero = jnp.zeros_like(blocks[0])
-    even = [zero] + [pltpu.roll(b, HALO, 1) for b in blocks]
-    odd = [pltpu.roll(b, LANES - HALO, 1) for b in blocks] + [zero]
+def tiles_of(source):
+    return [source[:, k * LANES : (k + 1) * LANES] for k in range(source.shape[1] // LANES)]
+
+
+def windows(tiles, lane):
+    zero = jnp.zeros_like(tiles[0])
+    even = [zero] + [pltpu.roll(tile, HALO, 1) for tile in tiles]
+    odd = [pltpu.roll(tile, LANES - OWN + HALO, 1) for tile in tiles] + [zero]
     out = []
-    for k in range(len(blocks)):
+    for k in range(len(tiles)):
         out.append(jnp.where(lane < HALO, even[k], even[k + 1]))
-        out.append(jnp.where(lane < LANES - HALO, odd[k], odd[k + 1]))
+        out.append(jnp.where(lane < LANES - OWN + HALO, odd[k], odd[k + 1]))
     return out
 
 
-def spread(sources, out, plane):
-    lane = lax.broadcasted_iota(jnp.int32, (ROWS, LANES), 1)
-    for source in sources:
-        blocks = [source[:, k * LANES : (k + 1) * LANES] for k in range(source.shape[1] // LANES)]
-        for peer, window in enumerate(windows(blocks, lane)):
-            out[peer, plane] = window
-        plane += 1
+def riders(tiles, lane):
+    zero = jnp.zeros_like(tiles[0])
+    turned = {shift: [pltpu.roll(tile, shift, 1) for tile in tiles] for shift in (16, 48, 80, 112)}
+    edge = [zero] + turned[112] + [zero]
+    out = []
+    for k in range(len(tiles)):
+        out.append([jnp.where(lane < 112, edge[k], edge[k + 1]), turned[80][k], turned[48][k]])
+        out.append([turned[48][k], turned[16][k], jnp.where(lane < 112, edge[k + 1], edge[k + 2])])
+    return out
+
+
+def put(out, peer, plane, value):
+    out[peer, 2 * plane] = value[:HALF]
+    out[peer, 2 * plane + 1] = value[HALF:]
 
 
 def own_kernel(now, terms, out):
     core = lax.axis_index("c")
-    spread([now.at[0], terms.at[2 * core], terms.at[1 + core]], out, 0)
+    lane = lax.broadcasted_iota(jnp.int32, (ROWS, LANES), 1)
+    fields = windows(tiles_of(now.at[0]), lane)
+    parts = riders(tiles_of(terms.at[2 * core]), lane)
+    across = windows(tiles_of(terms.at[1]), lane)
+    upper = (lane >= 0) & (core == 0)
+    for peer, (field, part, drift) in enumerate(zip(fields, parts, across)):
+        put(out, peer, 0, jnp.where(lane < WIDE, field, part[0]))
+        put(out, peer, 1, part[1])
+        put(out, peer, 2, part[2])
+        out[peer, 6] = jnp.where(upper[:HALF], drift[:HALF], drift[HALF:])
 
 
 def pack_kernel(own, before, earlier, out):
+    lane = lax.broadcasted_iota(jnp.int32, (ROWS, LANES), 1)
+    narrow = lane[:HALF] < WIDE
     for peer in range(out.shape[0]):
-        for plane in range(3):
-            out[peer, plane] = own[peer, plane]
-    spread([before.at[0], earlier.at[0]], out, 3)
+        for half in (0, 1, 6):
+            out[peer, half] = own[peer, half]
+    for plane, source in ((1, before), (2, earlier)):
+        for peer, window in enumerate(windows(tiles_of(source.at[0]), lane)):
+            out[peer, 2 * plane] = jnp.where(narrow, window[:HALF], own[peer, 2 * plane])
+            out[peer, 2 * plane + 1] = jnp.where(narrow, window[HALF:], own[peer, 2 * plane + 1])
 
 
 def krylov_kernel(strips, polynomial, got, out, coef, k0, k1, k2, k3, k4, z1, z2, z3, z4, work_x, work_y):
@@ -70,14 +97,25 @@
             ref[t, PAD + rows :] = edge
 
     for s in range(strips):
+        for c in range(2):
+            peer = c * strips + s
+            at = PAD + s * ROWS
+            for plane in range(3):
+                k0[times - 2 + c - 2 * plane, at : at + HALF] = got[peer, 2 * plane]
+                k0[times - 2 + c - 2 * plane, at + HALF : at + ROWS] = got[peer, 2 * plane + 1]
+            coef[3, s * ROWS + c * HALF : s * ROWS + (c + 1) * HALF] = got[peer, 6]
+
+    def rider(at, c):
+        last = [pltpu.roll(k0[times - 2 + c - 2 * plane, at], 32 * (plane + 1), 1) for plane in range(3)]
+        last[2] = jnp.where(lane < WIDE, last[2], 0.0)
+        return jnp.where(lane < 32, last[0], jnp.where(lane < 64, last[1], last[2]))
+
+    for s in range(strips):
         there = slice(s * ROWS, (s + 1) * ROWS)
         inner = slice(PAD + s * ROWS, PAD + (s + 1) * ROWS)
-        for c in range(2):
-            for plane in range(3):
-                k0[times - 2 + c - 2 * plane, inner] = got[c * strips + s, (0, 3, 4)[plane]]
-        diffuse = got[s, 1]
-        half_x = 0.5 * got[s, 2]
-        half_y = 0.5 * got[strips + s, 1]
+        diffuse = rider(inner, 0)
+        half_x = 0.5 * coef[3, there]
+        half_y = 0.5 * rider(inner, 1)
         north = -diffuse - half_y
         south = half_y - diffuse
         if s == 0:
@@ -158,7 +196,7 @@
         value = jnp.sum(jnp.where(mine, total, 0.0), axis=0, keepdims=True)
         value = jnp.sum(value, axis=1, keepdims=True)
         packed = packed + jnp.where(lane[0:1] == n, value, 0.0)
-    packed = jnp.where(row == 0, packed, 0.0)
+    packed = jnp.where(row[:HALF] == 0, packed, 0.0)
 
     for c in range(2):
         for s in range(strips):
@@ -167,10 +205,9 @@
             for pair in range(2):
                 low = lifted[2 * pair]
                 high = lifted[2 * pair + 1]
-                left = pltpu.roll(low[low.shape[0] - 2 + c, at], LANES - HALO, 1)
-                right = pltpu.roll(high[high.shape[0] - 2 + c, at], HALO, 1)
-                out[peer, pair] = jnp.where(lane < OWN, left, right)
-            out[peer, 2] = packed
+                turned = pltpu.roll(high[high.shape[0] - 2 + c, at], OWN, 1)
+                put(out, peer, pair, jnp.where(mine, low[low.shape[0] - 2 + c, at], turned))
+            out[peer, 4] = packed
 
 
 def least_squares(columns, beta_norm):
@@ -253,15 +290,19 @@
     weights, norms = cycle(gram)
     for n, norm in enumerate(norms):
         history[n] = jnp.max(norm)
-    low = jnp.where(lane < OWN, weights[0], weights[1])
-    high = jnp.where(lane < OWN, weights[2], weights[3])
-
-    def block(index):
-        value = low * got[index, 0] + high * got[index, 1]
-        return value + pltpu.roll(value, OWN, 1)
+    half = lane[:HALF]
+    mine = (half >= HALO) & (half < HALO + OWN)
+    low = jnp.where(mine, weights[0], weights[1])
+    high = jnp.where(mine, weights[2], weights[3])
+
+    def block(index, part):
+        value = low * got[index, part] + high * got[index, 2 + part]
+        return pltpu.roll(value, LANES - HALO, 1) + pltpu.roll(value, OWN - HALO, 1)
 
     for k in range(got.shape[0] // 2):
-        solution[0, :, k * LANES : (k + 1) * LANES] = jnp.where(lane < OWN, block(2 * k), block(2 * k + 1))
+        for part in range(2):
+            value = jnp.where(half < OWN, block(2 * k, part), block(2 * k + 1, part))
+            solution[0, part * HALF : (part + 1) * HALF, k * LANES : (k + 1) * LANES] = value
 
 
 def body(layers, strips, right_side, cell_terms, polynomial):
@@ -273,7 +314,7 @@
     before = lax.ppermute(right_side, "z", [(i, i + 1) for i in range(layers - 1)])
     own = pl.pallas_call(
         own_kernel,
-        out_shape=jax.ShapeDtypeStruct((peers, 3, ROWS, LANES), f32),
+        out_shape=jax.ShapeDtypeStruct((peers, 7, HALF, LANES), f32),
         in_specs=[VMEM] * 2,
         out_specs=VMEM,
         compiler_params=PARAMS,
@@ -282,7 +323,7 @@
     )(right_side, cell_terms)
     sent = pl.pallas_call(
         pack_kernel,
-        out_shape=jax.ShapeDtypeStruct((peers, 5, ROWS, LANES), f32),
+        out_shape=jax.ShapeDtypeStruct((peers, 7, HALF, LANES), f32),
         in_specs=[VMEM] * 3,
         out_specs=VMEM,
         compiler_params=PARAMS,
@@ -293,7 +334,7 @@
     field = lambda count: pltpu.VMEM((count, rows + 2 * PAD, LANES), f32)
     sent = pl.pallas_call(
         functools.partial(krylov_kernel, strips),
-        out_shape=jax.ShapeDtypeStruct((peers, 3, ROWS, LANES), f32),
+        out_shape=jax.ShapeDtypeStruct((peers, 5, HALF, LANES), f32),
         in_specs=[SMEM, VMEM],
         out_specs=VMEM,
         scratch_shapes=[pltpu.VMEM((5, rows, LANES), f32)]
@@ -304,7 +345,7 @@
         name="krylov",
     )(polynomial, got)
     got = lax.all_to_all(sent, layer, 0, 0, tiled=True)
-    partial = jnp.sum(got[:, 2, 0:1, :], axis=0)
+    partial = jnp.sum(got[:, 4, 0:1, :], axis=0)
     partial = jnp.broadcast_to(partial[None], (layers, 1, LANES))
     partial = lax.all_to_all(partial, "z", 0, 0, tiled=True)
     return pl.pallas_call(

time: 77.7 us -> 75.1 us (0.967)
  blocking collectives: 60.7 us -> 57.9 us
    all_to_all x2, blocking collectives: 34.9 us -> 32.1 us  [body(): got = lax.all_to_all(sent, layer, 0, 0, tiled=True)]
where the time goes in v3:
time: 75.1 us; the launch traced here: 74.7 us
  blocking collectives  57.9 us (77%)
  starting transfers between devices  9.27 us (12%)
  Pallas kernels  5.04 us (7%)
  local copies, waits for them, and re-layouts  1.77 us (2%)
    all_to_all x2, blocking collectives, body(): got = lax.all_to_all(sent, layer, 0, 0, tiled=True)  32.1 us
    all_to_all x1, blocking collectives, body(): partial = lax.all_to_all(partial, 'z', 0, 0, tiled=True)  25.8 us
    ppermute x1, starting transfers between devices, body(): lax.ppermute(right_side, 'z', [(i, i + 2) for i in range(layers - 2)])  5.73 us
    ppermute x1, starting transfers between devices, body(): lax.ppermute(right_side, 'z', [(i, i + 1) for i in range(layers - 1)])  3.54 us
    pallas_call x1, Pallas kernels, body(): pl.pallas_call(functools.partial(krylov_kernel, strips), out_shape=jax.Sh...  3.5 us
    unnamed x6, local copies, waits for them, and re-layouts  1.77 us
  transfers between devices with their start and end apart: 2, of which 0 were waited for; matrix products, arithmetic and copies ran while one was open for 0% of the time, Pallas kernels for 0%

profile of v3, /device:TPU:1, one launch (start us, length us, event | category | flops | bytes accessed | tf_op | source)
XLA Modules:
  0.0 74.7 jit_solution(14952104013166277501)
XLA Ops:
  0.6 5.7 %collective-permute-start.1 = (f32[1,8,2048]{2,1,0:T(8,128)}, f32[1,8,2048]{2,1,0:T(8,128)S(1)}, u32[]{:S(2)}, u32[]{:S(2)}) collective-permute-start(f32[1,8,2048]{2,1,0:T(8,128)} %now.1), channel_id=1, source_target_pairs={{0,64},{32,96},{64,128},{96,160},{128,192},{160,224},{192,256},{22... | collective-permute-start | bytes 196616 | tf_op jit(solution)/shard_map/ppermute | solution.py:313
  6.4 3.5 %collective-permute-start = (f32[1,8,2048]{2,1,0:T(8,128)}, f32[1,8,2048]{2,1,0:T(8,128)S(1)}, u32[]{:S(2)}, u32[]{:S(2)}) collective-permute-start(f32[1,8,2048]{2,1,0:T(8,128)} %now.1), channel_id=1, source_target_pairs={{0,32},{32,64},{64,96},{96,128},{128,160},{160,192},{192,224},{224... | collective-permute-start | bytes 196616 | tf_op jit(solution)/shard_map/ppermute | solution.py:314
  9.9 0.0 copy-start
  9.9 0.9 %copy-done = f32[3,8,2048]{2,1,0:T(8,128)S(1)} copy-done((f32[3,8,2048]{2,1,0:T(8,128)S(1)}, f32[3,8,2048]{2,1,0:T(8,128)}, u32[]{:S(2)}) %copy-start) | copy-done | bytes 196632
  10.8 0.0 copy-start.1
  10.8 0.8 %copy-done.1 = f32[1,8,2048]{2,1,0:T(8,128)S(1)} copy-done((f32[1,8,2048]{2,1,0:T(8,128)S(1)}, f32[1,8,2048]{2,1,0:T(8,128)}, u32[]{:S(2)}) %copy-start.1) | copy-done | bytes 65560
  11.7 0.2 own.1
  11.9 0.0 collective-permute-done.1.earlier
  11.9 0.0 collective-permute-done.before
  11.9 0.1 pack.1
  12.1 0.0 copy-start.2
  12.1 18.9 %all_to_all.15.got = f32[32,7,4,128]{3,2,1,0:T(4,128)S(1)} all-to-all(f32[32,7,4,128]{3,2,1,0:T(4,128)S(1)} %pack.1), channel_id=1, replica_groups=mesh['z'=16,'c'=2,'s'=16] {'c','s'}, dimensions={0} | all-to-all | bytes 917504 | tf_op jit(solution)/shard_map/all_to_all | solution.py:332
  30.9 0.0 copy-done.2
  30.9 3.5 %krylov.1 = f32[32,5,4,128]{3,2,1,0:T(4,128)S(1)} custom-call(f32[4]{0:T(128)S(1)} %copy-done.2, f32[32,7,4,128]{3,2,1,0:T(4,128)S(1)} %all_to_all.15.got), custom_call_target="tpu_custom_call" | custom-call | tf_op jit(solution)/shard_map/krylov/pallas_call | solution.py:335
  34.4 13.3 %all_to_all.16.got = f32[32,5,4,128]{3,2,1,0:T(4,128)S(1)} all-to-all(f32[32,5,4,128]{3,2,1,0:T(4,128)S(1)} %krylov.1), channel_id=1, replica_groups=mesh['z'=16,'c'=2,'s'=16] {'c','s'}, dimensions={0} | all-to-all | bytes 655360 | tf_op jit(solution)/shard_map/all_to_all | solution.py:347
  47.8 25.8 %all_to_all.17.partial = f32[16,1,128]{2,1,0:T(1,128)S(1)} all-to-all(f32[16,1,128]{2,1,0:T(1,128)S(1)} %broadcast_in_dim.2), channel_id=1, replica_groups=mesh['z'=16,'c'=2,'s'=16] {'z'}, dimensions={0} | all-to-all | bytes 16384 | tf_op jit(solution)/shard_map/all_to_all | solution.py:350
  73.5 1.2 %combine.1 = (f32[1,8,2048]{2,1,0:T(8,128)}, f32[4]{0:T(128)}) custom-call(f32[16,1,128]{2,1,0:T(1,128)S(1)} %all_to_all.17.partial, f32[32,5,4,128]{3,2,1,0:T(4,128)S(1)} %all_to_all.16.got), custom_call_target="tpu_custom_call" | custom-call | tf_op jit(solution)/shard_map/combine/pallas_call | solution.py:351
  (2 shorter events, 0.1 us)
Async XLA Ops:
  0.6 11.3 %collective-permute-start.1 = (f32[1,8,2048]{2,1,0:T(8,128)}, f32[1,8,2048]{2,1,0:T(8,128)S(1)}, u32[]{:S(2)}, u32[]{:S(2)}) collective-permute-start(f32[1,8,2048]{2,1,0:T(8,128)} %now.1), channel_id=1, source_target_pairs={{0,64},{32,96},{64,128},{96,160},{128,192},{160,224},{192,256},{22... | collective-permute-start | bytes 196616 | tf_op jit(solution)/shard_map/ppermute | solution.py:313
  6.4 5.5 %collective-permute-start = (f32[1,8,2048]{2,1,0:T(8,128)}, f32[1,8,2048]{2,1,0:T(8,128)S(1)}, u32[]{:S(2)}, u32[]{:S(2)}) collective-permute-start(f32[1,8,2048]{2,1,0:T(8,128)} %now.1), channel_id=1, source_target_pairs={{0,32},{32,64},{64,96},{96,128},{128,160},{160,192},{192,224},{224... | collective-permute-start | bytes 196616 | tf_op jit(solution)/shard_map/ppermute | solution.py:314
  9.9 0.9 %copy-start = (f32[3,8,2048]{2,1,0:T(8,128)S(1)}, f32[3,8,2048]{2,1,0:T(8,128)}, u32[]{:S(2)}) copy-start(f32[3,8,2048]{2,1,0:T(8,128)} %terms.1) | copy-start | bytes 589828
  10.8 0.8 %copy-start.1 = (f32[1,8,2048]{2,1,0:T(8,128)S(1)}, f32[1,8,2048]{2,1,0:T(8,128)}, u32[]{:S(2)}) copy-start(f32[1,8,2048]{2,1,0:T(8,128)} %now.1) | copy-start | bytes 196612
  12.1 18.9 %copy-start.2 = (f32[4]{0:T(128)S(1)}, f32[4]{0:T(128)}, u32[]{:S(2)}) copy-start(f32[4]{0:T(128)} %polynomial.1) | copy-start | bytes 52

commit v4 on v3

--- a/solution.py
+++ b/solution.py
@@ -77,6 +77,49 @@
         for peer, window in enumerate(windows(tiles_of(source.at[0]), lane)):
             out[peer, 2 * plane] = jnp.where(narrow, window[:HALF], own[peer, 2 * plane])
             out[peer, 2 * plane + 1] = jnp.where(narrow, window[HALF:], own[peer, 2 * plane + 1])
+
+
+def two_sum(a, b):
+    total = a + b
+    moved = total - a
+    return total, (a - (total - moved)) + (b - moved)
+
+
+def split(a):
+    scaled = 4097.0 * a
+    upper = scaled - (scaled - a)
+    return upper, a - upper
+
+
+def exact_sum(top, low, axis):
+    quantum = 1024.0 * jnp.max(jnp.abs(top), axis=axis, keepdims=True)
+    upper = (top + quantum) - quantum
+    rest = (top - upper) + low
+    return jnp.sum(upper, axis=axis, keepdims=True), jnp.sum(rest, axis=axis, keepdims=True)
+
+
+class Pair:
+    def __init__(self, top, low):
+        self.top = top + low
+        self.low = low - (self.top - top)
+        self.parts = split(self.top)
+
+    def times(self, other):
+        value = self.top * other.top
+        (a, b), (c, d) = self.parts, other.parts
+        error = (((a * c - value) + a * d) + b * c) + b * d
+        return Pair(value, error + (self.top * other.low + self.low * other.top))
+
+    def minus(self, other):
+        value, error = two_sum(self.top, -other.top)
+        return Pair(value, error + (self.low - other.low))
+
+    def inverse(self):
+        guess = 1.0 / self.top
+        value = guess * self.top
+        (a, b), (c, d) = split(guess), self.parts
+        error = (((a * c - value) + a * d) + b * c) + b * d
+        return Pair(guess, guess * (((1.0 - value) - error) - guess * self.low))
 
 
 def krylov_kernel(strips, polynomial, got, out, coef, k0, k1, k2, k3, k4, z1, z2, z3, z4, work_x, work_y):
@@ -177,26 +220,39 @@
         sweep(count, third)
         sweep(count - 1, fourth)
 
-    sums = [jnp.zeros((ROWS, LANES), jnp.float32) for _ in PAIRS]
+    mine = (lane >= HALO) & (lane < HALO + OWN)
+    nothing = jnp.zeros((ROWS, LANES), jnp.float32)
 
     def gram(index, sums):
         at = pl.ds(pl.multiple_of(index * ROWS, ROWS) + PAD, ROWS)
-        sums = list(sums)
-        for own in range(2):
-            vectors = [ref[ref.shape[0] - 2 + own, at] for ref in krylov]
-            for n, (i, j) in enumerate(PAIRS):
-                sums[n] = sums[n] + vectors[i] * vectors[j]
-        return tuple(sums)
-
-    sums = lax.fori_loop(0, strips, gram, tuple(sums))
-    row = lax.broadcasted_iota(jnp.int32, (ROWS, LANES), 0)
-    mine = (lane >= HALO) & (lane < HALO + OWN)
-    packed = jnp.zeros((1, LANES), jnp.float32)
-    for n, total in enumerate(sums):
-        value = jnp.sum(jnp.where(mine, total, 0.0), axis=0, keepdims=True)
-        value = jnp.sum(value, axis=1, keepdims=True)
-        packed = packed + jnp.where(lane[0:1] == n, value, 0.0)
-    packed = jnp.where(row[:HALF] == 0, packed, 0.0)
+        vectors = []
+        for ref in krylov:
+            newest = pltpu.roll(ref[ref.shape[0] - 1, at], OWN, 1)
+            value = jnp.where(mine, ref[ref.shape[0] - 2, at], newest)
+            vectors.append((value,) + split(value))
+        out = []
+        for (i, j), (top, low) in zip(PAIRS, sums):
+            (_, upper, lower), (other, other_upper, other_lower) = vectors[i], vectors[j]
+            top, error = two_sum(top, upper * other_upper)
+            out.append((top, low + (error + (upper * other_lower + lower * other))))
+        return tuple(out)
+
+    sums = lax.fori_loop(0, strips, gram, tuple((nothing, nothing) for _ in PAIRS))
+    tops = [nothing, nothing]
+    lows = [nothing, nothing]
+    for n, (top, low) in enumerate(sums):
+        for shift in (4, 2, 1):
+            top, error = two_sum(top, pltpu.roll(top, shift, 0))
+            low = low + pltpu.roll(low, shift, 0) + error
+        tops[n // ROWS] = jnp.where(sub == n % ROWS, top, tops[n // ROWS])
+        lows[n // ROWS] = jnp.where(sub == n % ROWS, low, lows[n // ROWS])
+    packed = [nothing, nothing]
+    for n in range(2):
+        parts = exact_sum(tops[n], lows[n], 1)
+        for kind in range(2):
+            packed[kind] = jnp.where(lane == sub + n * ROWS, parts[kind], packed[kind])
+    packed = [jnp.sum(value, axis=0, keepdims=True) for value in packed]
+    packed = jnp.where(sub[:HALF] == 0, packed[0], jnp.where(sub[:HALF] == 1, packed[1], 0.0))
 
     for c in range(2):
         for s in range(strips):
@@ -246,47 +302,73 @@
 
 
 def cycle(gram):
-    def product(left, right):
-        total = None
-        for i, a in enumerate(left):
-            for j, b in enumerate(right):
-                term = a * b * gram[min(i, j), max(i, j)]
-                total = term if total is None else total + term
-        return total
-
-    beta_norm = jnp.sqrt(gram[0, 0])
-    basis = [[1.0 / beta_norm]]
+    size = KRYLOV + 1
+    floors = [1e-12 * gram[k, k].top + 1e-30 for k in range(size)]
+    upper = {}
+    for k in range(size):
+        pivot = jnp.maximum(gram[k, k].top, floors[k])
+        root = jnp.sqrt(pivot)
+        upper[k, k] = root
+        for j in range(k + 1, size):
+            upper[k, j] = gram[k, j].top / root
+        if k + 1 < size:
+            inverse = Pair(pivot, jnp.where(gram[k, k].top < floors[k], 0.0, gram[k, k].low)).inverse()
+            for i in range(k + 1, size):
+                factor = gram[k, i].times(inverse)
+                for j in range(i, size):
+                    gram[i, j] = gram[i, j].minus(factor.times(gram[k, j]))
+
+    mapped = []
+    for i in range(KRYLOV):
+        column = []
+        for row in range(i + 2):
+            value = upper[row, i + 1]
+            if row <= i:
+                value = value + upper[row, i]
+            for k in range(max(row - 1, 0), i):
+                value = value - upper[k, i] * mapped[k][row]
+            column.append(value / upper[i, i])
+        mapped.append(column)
+
+    beta_norm = upper[0, 0]
+    basis = [[jnp.ones_like(beta_norm)]]
     columns = []
     for at in range(KRYLOV):
         newest = basis[-1]
-        image = list(newest) + [None]
-        for m, value in enumerate(newest):
-            image[m + 1] = value if image[m + 1] is None else image[m + 1] + value
-        projections = [product(image, vector) for vector in basis]
+        image = []
+        for row in range(at + 2):
+            terms = [mapped[i][row] * newest[i] for i in range(max(row - 1, 0), at + 1)]
+            image.append(functools.reduce(lambda a, b: a + b, terms))
+        projections = []
         rest = list(image)
+        for vector in basis:
+            terms = [a * b for a, b in zip(image, vector)]
+            projections.append(functools.reduce(lambda a, b: a + b, terms))
         for vector, weight in zip(basis, projections):
-            for m, value in enumerate(vector):
-                rest[m] = rest[m] - weight * value
-        length = jnp.sqrt(jnp.maximum(product(rest, rest), 0.0) + 1e-06)
+            for row, value in enumerate(vector):
+                rest[row] = rest[row] - weight * value
+        terms = [value * value for value in rest]
+        length = jnp.sqrt(functools.reduce(lambda a, b: a + b, terms) + 1e-06)
         columns.append(projections + [length])
         basis.append([value / length for value in rest])
     solved, history = least_squares(columns, beta_norm)
-    weights = []
-    for m in range(KRYLOV):
-        total = None
-        for j in range(m, KRYLOV):
-            term = solved[j] * basis[j][m]
-            total = term if total is None else total + term
-        weights.append(total)
+    weights = [None] * KRYLOV
+    for row in reversed(range(KRYLOV)):
+        terms = [solved[j] * basis[j][row] for j in range(row, KRYLOV)]
+        value = functools.reduce(lambda a, b: a + b, terms)
+        for later in range(row + 1, KRYLOV):
+            value = value - upper[row, later] * weights[later]
+        weights[row] = value / upper[row, row]
     return weights, history
 
 
 def combine_kernel(partial, got, solution, history):
     lane = lax.broadcasted_iota(jnp.int32, (ROWS, LANES), 1)
-    total = jnp.sum(partial[:, 0, :], axis=0, keepdims=True)
+    top, low = exact_sum(partial[:, 0, :], partial[:, 1, :], 0)
     gram = {}
     for n, pair in enumerate(PAIRS):
-        gram[pair] = jnp.sum(jnp.where(lane[0:1] == n, total, 0.0), axis=1, keepdims=True)
+        values = [jnp.sum(jnp.where(lane[0:1] == n, row, 0.0), axis=1, keepdims=True) for row in (top, low)]
+        gram[pair] = Pair(*values)
     weights, norms = cycle(gram)
     for n, norm in enumerate(norms):
         history[n] = jnp.max(norm)
@@ -345,8 +427,8 @@
         name="krylov",
     )(polynomial, got)
     got = lax.all_to_all(sent, layer, 0, 0, tiled=True)
-    partial = jnp.sum(got[:, 4, 0:1, :], axis=0)
-    partial = jnp.broadcast_to(partial[None], (layers, 1, LANES))
+    partial = jnp.concatenate(exact_sum(got[:, 4, 0, :], got[:, 4, 1, :], 0))
+    partial = jnp.broadcast_to(partial[None], (layers, 2, LANES))
     partial = lax.all_to_all(partial, "z", 0, 0, tiled=True)
     return pl.pallas_call(
         combine_kernel,

time: 75.1 us -> 76.8 us (1.023)
  Pallas kernels: 5.04 us -> 6.61 us
    pallas_call x1, Pallas kernels: 3.5 us -> 5.03 us  [body(): pl.pallas_call(functools.partial(krylov_kernel, strips), out_shape=jax.Sh...]
where the time goes in v4:
time: 76.8 us; the launch traced here: 76.5 us
  blocking collectives  58 us (76%)
  starting transfers between devices  9.27 us (12%)
  Pallas kernels  6.61 us (9%)
  local copies, waits for them, and re-layouts  1.8 us (2%)
    all_to_all x2, blocking collectives, body(): got = lax.all_to_all(sent, layer, 0, 0, tiled=True)  32.1 us
    all_to_all x1, blocking collectives, body(): partial = lax.all_to_all(partial, 'z', 0, 0, tiled=True)  25.9 us
    ppermute x1, starting transfers between devices, body(): lax.ppermute(right_side, 'z', [(i, i + 2) for i in range(layers - 2)])  5.73 us
    pallas_call x1, Pallas kernels, body(): pl.pallas_call(functools.partial(krylov_kernel, strips), out_shape=jax.Sh...  5.03 us
    ppermute x1, starting transfers between devices, body(): lax.ppermute(right_side, 'z', [(i, i + 1) for i in range(layers - 1)])  3.54 us
    unnamed x6, local copies, waits for them, and re-layouts  1.77 us
  transfers between devices with their start and end apart: 2, of which 0 were waited for; matrix products, arithmetic and copies ran while one was open for 0% of the time, Pallas kernels for 0%

profile of v4, /device:TPU:1, one launch (start us, length us, event | category | flops | bytes accessed | tf_op | source)
XLA Modules:
  0.0 76.5 jit_solution(3302913467061519860)
XLA Ops:
  0.6 5.7 %collective-permute-start.1 = (f32[1,8,2048]{2,1,0:T(8,128)}, f32[1,8,2048]{2,1,0:T(8,128)S(1)}, u32[]{:S(2)}, u32[]{:S(2)}) collective-permute-start(f32[1,8,2048]{2,1,0:T(8,128)} %now.1), channel_id=1, source_target_pairs={{0,64},{32,96},{64,128},{96,160},{128,192},{160,224},{192,256},{22... | collective-permute-start | bytes 196616 | tf_op jit(solution)/shard_map/ppermute | solution.py:395
  6.4 3.5 %collective-permute-start = (f32[1,8,2048]{2,1,0:T(8,128)}, f32[1,8,2048]{2,1,0:T(8,128)S(1)}, u32[]{:S(2)}, u32[]{:S(2)}) collective-permute-start(f32[1,8,2048]{2,1,0:T(8,128)} %now.1), channel_id=1, source_target_pairs={{0,32},{32,64},{64,96},{96,128},{128,160},{160,192},{192,224},{224... | collective-permute-start | bytes 196616 | tf_op jit(solution)/shard_map/ppermute | solution.py:396
  9.9 0.0 copy-start
  9.9 0.9 %copy-done = f32[3,8,2048]{2,1,0:T(8,128)S(1)} copy-done((f32[3,8,2048]{2,1,0:T(8,128)S(1)}, f32[3,8,2048]{2,1,0:T(8,128)}, u32[]{:S(2)}) %copy-start) | copy-done | bytes 196632
  10.8 0.0 copy-start.1
  10.8 0.8 %copy-done.1 = f32[1,8,2048]{2,1,0:T(8,128)S(1)} copy-done((f32[1,8,2048]{2,1,0:T(8,128)S(1)}, f32[1,8,2048]{2,1,0:T(8,128)}, u32[]{:S(2)}) %copy-start.1) | copy-done | bytes 65560
  11.7 0.2 own.1
  11.9 0.0 collective-permute-done.1.earlier
  11.9 0.0 collective-permute-done.before
  11.9 0.1 pack.1
  12.1 0.0 copy-start.2
  12.1 18.9 %all_to_all.15.got = f32[32,7,4,128]{3,2,1,0:T(4,128)S(1)} all-to-all(f32[32,7,4,128]{3,2,1,0:T(4,128)S(1)} %pack.1), channel_id=1, replica_groups=mesh['z'=16,'c'=2,'s'=16] {'c','s'}, dimensions={0} | all-to-all | bytes 917504 | tf_op jit(solution)/shard_map/all_to_all | solution.py:414
  30.9 0.0 copy-done.2
  30.9 5.0 %krylov.1 = f32[32,5,4,128]{3,2,1,0:T(4,128)S(1)} custom-call(f32[4]{0:T(128)S(1)} %copy-done.2, f32[32,7,4,128]{3,2,1,0:T(4,128)S(1)} %all_to_all.15.got), custom_call_target="tpu_custom_call" | custom-call | tf_op jit(solution)/shard_map/krylov/pallas_call | solution.py:417
  36.0 13.3 %all_to_all.16.got = f32[32,5,4,128]{3,2,1,0:T(4,128)S(1)} all-to-all(f32[32,5,4,128]{3,2,1,0:T(4,128)S(1)} %krylov.1), channel_id=1, replica_groups=mesh['z'=16,'c'=2,'s'=16] {'c','s'}, dimensions={0} | all-to-all | bytes 655360 | tf_op jit(solution)/shard_map/all_to_all | solution.py:429
  49.4 25.9 %all_to_all.17.partial = f32[16,2,128]{2,1,0:T(2,128)S(1)} all-to-all(f32[16,2,128]{2,1,0:T(2,128)S(1)} %broadcast_in_dim.15), channel_id=1, replica_groups=mesh['z'=16,'c'=2,'s'=16] {'z'}, dimensions={0} | all-to-all | bytes 32768 | tf_op jit(solution)/shard_map/all_to_all | solution.py:432
  75.2 1.2 %combine.1 = (f32[1,8,2048]{2,1,0:T(8,128)}, f32[4]{0:T(128)}) custom-call(f32[16,2,128]{2,1,0:T(2,128)S(1)} %all_to_all.17.partial, f32[32,5,4,128]{3,2,1,0:T(4,128)S(1)} %all_to_all.16.got), custom_call_target="tpu_custom_call" | custom-call | tf_op jit(solution)/shard_map/combine/pallas_call | solution.py:433
  (6 shorter events, 0.1 us)
Async XLA Ops:
  0.6 11.3 %collective-permute-start.1 = (f32[1,8,2048]{2,1,0:T(8,128)}, f32[1,8,2048]{2,1,0:T(8,128)S(1)}, u32[]{:S(2)}, u32[]{:S(2)}) collective-permute-start(f32[1,8,2048]{2,1,0:T(8,128)} %now.1), channel_id=1, source_target_pairs={{0,64},{32,96},{64,128},{96,160},{128,192},{160,224},{192,256},{22... | collective-permute-start | bytes 196616 | tf_op jit(solution)/shard_map/ppermute | solution.py:395
  6.4 5.5 %collective-permute-start = (f32[1,8,2048]{2,1,0:T(8,128)}, f32[1,8,2048]{2,1,0:T(8,128)S(1)}, u32[]{:S(2)}, u32[]{:S(2)}) collective-permute-start(f32[1,8,2048]{2,1,0:T(8,128)} %now.1), channel_id=1, source_target_pairs={{0,32},{32,64},{64,96},{96,128},{128,160},{160,192},{192,224},{224... | collective-permute-start | bytes 196616 | tf_op jit(solution)/shard_map/ppermute | solution.py:396
  9.9 0.9 %copy-start = (f32[3,8,2048]{2,1,0:T(8,128)S(1)}, f32[3,8,2048]{2,1,0:T(8,128)}, u32[]{:S(2)}) copy-start(f32[3,8,2048]{2,1,0:T(8,128)} %terms.1) | copy-start | bytes 589828
  10.8 0.8 %copy-start.1 = (f32[1,8,2048]{2,1,0:T(8,128)S(1)}, f32[1,8,2048]{2,1,0:T(8,128)}, u32[]{:S(2)}) copy-start(f32[1,8,2048]{2,1,0:T(8,128)} %now.1) | copy-start | bytes 196612
  12.1 18.9 %copy-start.2 = (f32[4]{0:T(128)S(1)}, f32[4]{0:T(128)}, u32[]{:S(2)}) copy-start(f32[4]{0:T(128)} %polynomial.1) | copy-start | bytes 52

commit v5 on v4

--- a/solution.py
+++ b/solution.py
@@ -15,7 +15,7 @@
 LANES = 128
 ROWS = 8
 PAD = 8
-CHUNK = 128
+CHUNK = 64
 PAIRS = [(i, j) for i in range(KRYLOV + 1) for j in range(i, KRYLOV + 1)]
 VMEM = pl.BlockSpec(memory_space=pltpu.VMEM)
 SMEM = pl.BlockSpec(memory_space=pltpu.SMEM)
@@ -122,7 +122,7 @@
         return Pair(guess, guess * (((1.0 - value) - error) - guess * self.low))
 
 
-def krylov_kernel(strips, polynomial, got, out, coef, k0, k1, k2, k3, k4, z1, z2, z3, z4, work_x, work_y):
+def krylov_kernel(strips, polynomial, got, out, coef, inner_coef, k0, k1, k2, k3, k4, z1, z2, z3, z4, work_x, work_y):
     rows = ROWS * strips
     times = KRYLOV + 2
     krylov = [k0, k1, k2, k3, k4]
@@ -170,61 +170,56 @@
         coef[2, there] = south
         coef[3, there] = jnp.where(first_col, 0.0, -diffuse - half_x)
         coef[4, there] = jnp.where(last_col, 0.0, half_x - diffuse)
-
-    def sweep(count, apply):
-        def step(index, carry):
-            at = pl.multiple_of(index * CHUNK, CHUNK)
-            parts = [coef[i, pl.ds(at, CHUNK)] for i in range(5)]
+        for i in range(5):
+            scaled = polynomial[3] * coef[i, there]
+            inner_coef[i, there] = polynomial[2] + scaled if i == 0 else scaled
+
+    def sweep(count, terms, apply):
+        chunk = min(CHUNK, rows)
+        for at in range(0, rows, chunk):
+            parts = [terms[i, at : at + chunk] for i in range(5)]
 
             def stencil(ref, t):
-                middle = ref[t, pl.ds(at + PAD, CHUNK)]
-                north = ref[t, pl.ds(at + PAD - 1, CHUNK)]
-                south = ref[t, pl.ds(at + PAD + 1, CHUNK)]
+                middle = ref[t, at + PAD : at + PAD + chunk]
+                north = ref[t, at + PAD - 1 : at + PAD - 1 + chunk]
+                south = ref[t, at + PAD + 1 : at + PAD + 1 + chunk]
                 west = pltpu.roll(middle, 1, 1)
                 east = pltpu.roll(middle, LANES - 1, 1)
-                value = (
+                return (
                     (parts[0] * middle + parts[3] * west)
                     + (parts[1] * north + parts[2] * south)
                     + parts[4] * east
                 )
-                return value, middle
 
             for t in range(count):
-                apply(t, pl.ds(at + PAD, CHUNK), stencil)
-            return carry
-
-        lax.fori_loop(0, rows // CHUNK, step, 0)
+                apply(t, slice(at + PAD, at + PAD + chunk), stencil)
 
     for j in range(KRYLOV):
         source, target, upper = krylov[j], krylov[j + 1], lifted[j]
         count = times - j
 
         def first(t, at, stencil):
-            value, middle = stencil(source, t)
-            work_x[t, at] = polynomial[2] * middle + polynomial[3] * value
+            work_x[t, at] = stencil(source, t)
 
         def second(t, at, stencil):
-            value, _ = stencil(work_x, t)
-            work_y[t, at] = polynomial[1] * source[t, at] + value
+            work_y[t, at] = polynomial[1] * source[t, at] + stencil(work_x, t)
 
         def third(t, at, stencil):
-            value, _ = stencil(work_y, t)
-            upper[t, at] = polynomial[0] * source[t, at] + value
+            upper[t, at] = polynomial[0] * source[t, at] + stencil(work_y, t)
 
         def fourth(t, at, stencil):
-            value, _ = stencil(upper, t + 1)
-            target[t, at] = value - upper[t, at] - source[t + 1, at]
-
-        sweep(count, first)
-        sweep(count, second)
-        sweep(count, third)
-        sweep(count - 1, fourth)
+            target[t, at] = stencil(upper, t + 1) - upper[t, at] - source[t + 1, at]
+
+        sweep(count, inner_coef, first)
+        sweep(count, coef, second)
+        sweep(count, coef, third)
+        sweep(count - 1, coef, fourth)
 
     mine = (lane >= HALO) & (lane < HALO + OWN)
     nothing = jnp.zeros((ROWS, LANES), jnp.float32)
 
     def gram(index, sums):
-        at = pl.ds(pl.multiple_of(index * ROWS, ROWS) + PAD, ROWS)
+        at = slice(PAD + index * ROWS, PAD + (index + 1) * ROWS)
         vectors = []
         for ref in krylov:
             newest = pltpu.roll(ref[ref.shape[0] - 1, at], OWN, 1)
@@ -235,9 +230,11 @@
             (_, upper, lower), (other, other_upper, other_lower) = vectors[i], vectors[j]
             top, error = two_sum(top, upper * other_upper)
             out.append((top, low + (error + (upper * other_lower + lower * other))))
-        return tuple(out)
-
-    sums = lax.fori_loop(0, strips, gram, tuple((nothing, nothing) for _ in PAIRS))
+        return out
+
+    sums = [(nothing, nothing) for _ in PAIRS]
+    for index in range(strips):
+        sums = gram(index, sums)
     tops = [nothing, nothing]
     lows = [nothing, nothing]
     for n, (top, low) in enumerate(sums):
@@ -419,7 +416,7 @@
         out_shape=jax.ShapeDtypeStruct((peers, 5, HALF, LANES), f32),
         in_specs=[SMEM, VMEM],
         out_specs=VMEM,
-        scratch_shapes=[pltpu.VMEM((5, rows, LANES), f32)]
+        scratch_shapes=[pltpu.VMEM((5, rows, LANES), f32)] * 2
         + [field(times - j) for j in range(KRYLOV + 1)]
         + [field(times - j) for j in range(KRYLOV)]
         + [field(times), field(times)],

time: 76.8 us -> 75.5 us (0.983)
  Pallas kernels: 6.61 us -> 5.29 us
    pallas_call x1, Pallas kernels: 5.03 us -> 3.72 us  [body(): pl.pallas_call(functools.partial(krylov_kernel, strips), out_shape=jax.Sh...]
where the time goes in v5:
time: 75.5 us; the launch traced here: 75.1 us
  blocking collectives  58 us (77%)
  starting transfers between devices  9.27 us (12%)
  Pallas kernels  5.29 us (7%)
  local copies, waits for them, and re-layouts  1.8 us (2%)
    all_to_all x2, blocking collectives, body(): got = lax.all_to_all(sent, layer, 0, 0, tiled=True)  32.1 us
    all_to_all x1, blocking collectives, body(): partial = lax.all_to_all(partial, 'z', 0, 0, tiled=True)  25.9 us
    ppermute x1, starting transfers between devices, body(): lax.ppermute(right_side, 'z', [(i, i + 2) for i in range(layers - 2)])  5.73 us
    pallas_call x1, Pallas kernels, body(): pl.pallas_call(functools.partial(krylov_kernel, strips), out_shape=jax.Sh...  3.72 us
    ppermute x1, starting transfers between devices, body(): lax.ppermute(right_side, 'z', [(i, i + 1) for i in range(layers - 1)])  3.54 us
    unnamed x6, local copies, waits for them, and re-layouts  1.77 us
  transfers between devices with their start and end apart: 2, of which 0 were waited for; matrix products, arithmetic and copies ran while one was open for 0% of the time, Pallas kernels for 0%

profile of v5, /device:TPU:1, one launch (start us, length us, event | category | flops | bytes accessed | tf_op | source)
XLA Modules:
  0.0 75.1 jit_solution(1199140601459973362)
XLA Ops:
  0.6 5.7 %collective-permute-start.1 = (f32[1,8,2048]{2,1,0:T(8,128)}, f32[1,8,2048]{2,1,0:T(8,128)S(1)}, u32[]{:S(2)}, u32[]{:S(2)}) collective-permute-start(f32[1,8,2048]{2,1,0:T(8,128)} %now.1), channel_id=1, source_target_pairs={{0,64},{32,96},{64,128},{96,160},{128,192},{160,224},{192,256},{22... | collective-permute-start | bytes 196616 | tf_op jit(solution)/shard_map/ppermute | solution.py:392
  6.4 3.5 %collective-permute-start = (f32[1,8,2048]{2,1,0:T(8,128)}, f32[1,8,2048]{2,1,0:T(8,128)S(1)}, u32[]{:S(2)}, u32[]{:S(2)}) collective-permute-start(f32[1,8,2048]{2,1,0:T(8,128)} %now.1), channel_id=1, source_target_pairs={{0,32},{32,64},{64,96},{96,128},{128,160},{160,192},{192,224},{224... | collective-permute-start | bytes 196616 | tf_op jit(solution)/shard_map/ppermute | solution.py:393
  9.9 0.0 copy-start
  9.9 0.9 %copy-done = f32[3,8,2048]{2,1,0:T(8,128)S(1)} copy-done((f32[3,8,2048]{2,1,0:T(8,128)S(1)}, f32[3,8,2048]{2,1,0:T(8,128)}, u32[]{:S(2)}) %copy-start) | copy-done | bytes 196632
  10.8 0.0 copy-start.1
  10.8 0.8 %copy-done.1 = f32[1,8,2048]{2,1,0:T(8,128)S(1)} copy-done((f32[1,8,2048]{2,1,0:T(8,128)S(1)}, f32[1,8,2048]{2,1,0:T(8,128)}, u32[]{:S(2)}) %copy-start.1) | copy-done | bytes 65560
  11.7 0.2 own.1
  11.9 0.0 collective-permute-done.1.earlier
  11.9 0.0 collective-permute-done.before
  11.9 0.1 pack.1
  12.1 0.0 copy-start.2
  12.1 18.9 %all_to_all.15.got = f32[32,7,4,128]{3,2,1,0:T(4,128)S(1)} all-to-all(f32[32,7,4,128]{3,2,1,0:T(4,128)S(1)} %pack.1), channel_id=1, replica_groups=mesh['z'=16,'c'=2,'s'=16] {'c','s'}, dimensions={0} | all-to-all | bytes 917504 | tf_op jit(solution)/shard_map/all_to_all | solution.py:411
  30.9 0.0 copy-done.2
  30.9 3.7 %krylov.1 = f32[32,5,4,128]{3,2,1,0:T(4,128)S(1)} custom-call(f32[4]{0:T(128)S(1)} %copy-done.2, f32[32,7,4,128]{3,2,1,0:T(4,128)S(1)} %all_to_all.15.got), custom_call_target="tpu_custom_call" | custom-call | tf_op jit(solution)/shard_map/krylov/pallas_call | solution.py:414
  34.7 13.3 %all_to_all.16.got = f32[32,5,4,128]{3,2,1,0:T(4,128)S(1)} all-to-all(f32[32,5,4,128]{3,2,1,0:T(4,128)S(1)} %krylov.1), channel_id=1, replica_groups=mesh['z'=16,'c'=2,'s'=16] {'c','s'}, dimensions={0} | all-to-all | bytes 655360 | tf_op jit(solution)/shard_map/all_to_all | solution.py:426
  48.0 25.9 %all_to_all.17.partial = f32[16,2,128]{2,1,0:T(2,128)S(1)} all-to-all(f32[16,2,128]{2,1,0:T(2,128)S(1)} %broadcast_in_dim.15), channel_id=1, replica_groups=mesh['z'=16,'c'=2,'s'=16] {'z'}, dimensions={0} | all-to-all | bytes 32768 | tf_op jit(solution)/shard_map/all_to_all | solution.py:429
  73.9 1.2 %combine.1 = (f32[1,8,2048]{2,1,0:T(8,128)}, f32[4]{0:T(128)}) custom-call(f32[16,2,128]{2,1,0:T(2,128)S(1)} %all_to_all.17.partial, f32[32,5,4,128]{3,2,1,0:T(4,128)S(1)} %all_to_all.16.got), custom_call_target="tpu_custom_call" | custom-call | tf_op jit(solution)/shard_map/combine/pallas_call | solution.py:430
  (6 shorter events, 0.1 us)
Async XLA Ops:
  0.6 11.3 %collective-permute-start.1 = (f32[1,8,2048]{2,1,0:T(8,128)}, f32[1,8,2048]{2,1,0:T(8,128)S(1)}, u32[]{:S(2)}, u32[]{:S(2)}) collective-permute-start(f32[1,8,2048]{2,1,0:T(8,128)} %now.1), channel_id=1, source_target_pairs={{0,64},{32,96},{64,128},{96,160},{128,192},{160,224},{192,256},{22... | collective-permute-start | bytes 196616 | tf_op jit(solution)/shard_map/ppermute | solution.py:392
  6.4 5.5 %collective-permute-start = (f32[1,8,2048]{2,1,0:T(8,128)}, f32[1,8,2048]{2,1,0:T(8,128)S(1)}, u32[]{:S(2)}, u32[]{:S(2)}) collective-permute-start(f32[1,8,2048]{2,1,0:T(8,128)} %now.1), channel_id=1, source_target_pairs={{0,32},{32,64},{64,96},{96,128},{128,160},{160,192},{192,224},{224... | collective-permute-start | bytes 196616 | tf_op jit(solution)/shard_map/ppermute | solution.py:393
  9.9 0.9 %copy-start = (f32[3,8,2048]{2,1,0:T(8,128)S(1)}, f32[3,8,2048]{2,1,0:T(8,128)}, u32[]{:S(2)}) copy-start(f32[3,8,2048]{2,1,0:T(8,128)} %terms.1) | copy-start | bytes 589828
  10.8 0.8 %copy-start.1 = (f32[1,8,2048]{2,1,0:T(8,128)S(1)}, f32[1,8,2048]{2,1,0:T(8,128)}, u32[]{:S(2)}) copy-start(f32[1,8,2048]{2,1,0:T(8,128)} %now.1) | copy-start | bytes 196612
  12.1 18.9 %copy-start.2 = (f32[4]{0:T(128)S(1)}, f32[4]{0:T(128)}, u32[]{:S(2)}) copy-start(f32[4]{0:T(128)} %polynomial.1) | copy-start | bytes 52

commit v6 on v5

--- a/solution.py
+++ b/solution.py
@@ -426,7 +426,8 @@
     got = lax.all_to_all(sent, layer, 0, 0, tiled=True)
     partial = jnp.concatenate(exact_sum(got[:, 4, 0, :], got[:, 4, 1, :], 0))
     partial = jnp.broadcast_to(partial[None], (layers, 2, LANES))
-    partial = lax.all_to_all(partial, "z", 0, 0, tiled=True)
+    order = [(layers // 2 + i) % layers for i in range(layers)]
+    partial = lax.all_to_all(partial, "z", 0, 0, axis_index_groups=[order], tiled=True)
     return pl.pallas_call(
         combine_kernel,
         out_shape=(jax.ShapeDtypeStruct(right_side.shape, f32), jax.ShapeDtypeStruct((KRYLOV,), f32)),

time: 75.5 us -> 68.1 us (0.902)
  blocking collectives: 58 us -> 50.7 us
    all_to_all x1, blocking collectives: 25.9 us -> 18.5 us  [body(): lax.all_to_all(partial, 'z', 0, 0, axis_index_groups=[order], tiled=True)]
where the time goes in v6:
time: 68.1 us; the launch traced here: 67.8 us
  blocking collectives  50.7 us (74%)
  starting transfers between devices  9.27 us (14%)
  Pallas kernels  5.29 us (8%)
  local copies, waits for them, and re-layouts  1.8 us (3%)
  between operations  0.71 us (1%)
    all_to_all x2, blocking collectives, body(): got = lax.all_to_all(sent, layer, 0, 0, tiled=True)  32.1 us
    all_to_all x1, blocking collectives, body(): lax.all_to_all(partial, 'z', 0, 0, axis_index_groups=[order], tiled=True)  18.5 us
    ppermute x1, starting transfers between devices, body(): lax.ppermute(right_side, 'z', [(i, i + 2) for i in range(layers - 2)])  5.73 us
    pallas_call x1, Pallas kernels, body(): pl.pallas_call(functools.partial(krylov_kernel, strips), out_shape=jax.Sh...  3.72 us
    ppermute x1, starting transfers between devices, body(): lax.ppermute(right_side, 'z', [(i, i + 1) for i in range(layers - 1)])  3.54 us
    unnamed x6, local copies, waits for them, and re-layouts  1.77 us
  transfers between devices with their start and end apart: 2, of which 0 were waited for; matrix products, arithmetic and copies ran while one was open for 0% of the time, Pallas kernels for 0%

profile of v6, /device:TPU:1, one launch (start us, length us, event | category | flops | bytes accessed | tf_op | source)
XLA Modules:
  0.0 67.8 jit_solution(2535846326763519024)
XLA Ops:
  0.6 5.7 %collective-permute-start.1 = (f32[1,8,2048]{2,1,0:T(8,128)}, f32[1,8,2048]{2,1,0:T(8,128)S(1)}, u32[]{:S(2)}, u32[]{:S(2)}) collective-permute-start(f32[1,8,2048]{2,1,0:T(8,128)} %now.1), channel_id=1, source_target_pairs={{0,64},{32,96},{64,128},{96,160},{128,192},{160,224},{192,256},{22... | collective-permute-start | bytes 196616 | tf_op jit(solution)/shard_map/ppermute | solution.py:392
  6.4 3.5 %collective-permute-start = (f32[1,8,2048]{2,1,0:T(8,128)}, f32[1,8,2048]{2,1,0:T(8,128)S(1)}, u32[]{:S(2)}, u32[]{:S(2)}) collective-permute-start(f32[1,8,2048]{2,1,0:T(8,128)} %now.1), channel_id=1, source_target_pairs={{0,32},{32,64},{64,96},{96,128},{128,160},{160,192},{192,224},{224... | collective-permute-start | bytes 196616 | tf_op jit(solution)/shard_map/ppermute | solution.py:393
  9.9 0.0 copy-start
  9.9 0.9 %copy-done = f32[3,8,2048]{2,1,0:T(8,128)S(1)} copy-done((f32[3,8,2048]{2,1,0:T(8,128)S(1)}, f32[3,8,2048]{2,1,0:T(8,128)}, u32[]{:S(2)}) %copy-start) | copy-done | bytes 196632
  10.8 0.0 copy-start.1
  10.8 0.8 %copy-done.1 = f32[1,8,2048]{2,1,0:T(8,128)S(1)} copy-done((f32[1,8,2048]{2,1,0:T(8,128)S(1)}, f32[1,8,2048]{2,1,0:T(8,128)}, u32[]{:S(2)}) %copy-start.1) | copy-done | bytes 65560
  11.7 0.2 own.1
  11.9 0.0 collective-permute-done.1.earlier
  11.9 0.0 collective-permute-done.before
  11.9 0.1 pack.1
  12.1 0.0 copy-start.2
  12.1 18.9 %all_to_all.15.got = f32[32,7,4,128]{3,2,1,0:T(4,128)S(1)} all-to-all(f32[32,7,4,128]{3,2,1,0:T(4,128)S(1)} %pack.1), channel_id=1, replica_groups=mesh['z'=16,'c'=2,'s'=16] {'c','s'}, dimensions={0} | all-to-all | bytes 917504 | tf_op jit(solution)/shard_map/all_to_all | solution.py:411
  30.9 0.0 copy-done.2
  30.9 3.7 %krylov.1 = f32[32,5,4,128]{3,2,1,0:T(4,128)S(1)} custom-call(f32[4]{0:T(128)S(1)} %copy-done.2, f32[32,7,4,128]{3,2,1,0:T(4,128)S(1)} %all_to_all.15.got), custom_call_target="tpu_custom_call" | custom-call | tf_op jit(solution)/shard_map/krylov/pallas_call | solution.py:414
  34.7 13.3 %all_to_all.16.got = f32[32,5,4,128]{3,2,1,0:T(4,128)S(1)} all-to-all(f32[32,5,4,128]{3,2,1,0:T(4,128)S(1)} %krylov.1), channel_id=1, replica_groups=mesh['z'=16,'c'=2,'s'=16] {'c','s'}, dimensions={0} | all-to-all | bytes 655360 | tf_op jit(solution)/shard_map/all_to_all | solution.py:426
  48.0 18.5 %all_to_all.17.partial = f32[16,2,128]{2,1,0:T(2,128)S(1)} all-to-all(f32[16,2,128]{2,1,0:T(2,128)S(1)} %broadcast_in_dim.15), channel_id=1, replica_groups={{256,288,320,352,384,416,448,480,0,32,64,96,128,160,192,224},{257,289,3..., dimensions={0} | all-to-all | bytes 32768 | tf_op jit(solution)/shard_map/all_to_all | solution.py:430
  66.6 1.2 %combine.1 = (f32[1,8,2048]{2,1,0:T(8,128)}, f32[4]{0:T(128)}) custom-call(f32[16,2,128]{2,1,0:T(2,128)S(1)} %all_to_all.17.partial, f32[32,5,4,128]{3,2,1,0:T(4,128)S(1)} %all_to_all.16.got), custom_call_target="tpu_custom_call" | custom-call | tf_op jit(solution)/shard_map/combine/pallas_call | solution.py:431
  (6 shorter events, 0.1 us)
Async XLA Ops:
  0.6 11.3 %collective-permute-start.1 = (f32[1,8,2048]{2,1,0:T(8,128)}, f32[1,8,2048]{2,1,0:T(8,128)S(1)}, u32[]{:S(2)}, u32[]{:S(2)}) collective-permute-start(f32[1,8,2048]{2,1,0:T(8,128)} %now.1), channel_id=1, source_target_pairs={{0,64},{32,96},{64,128},{96,160},{128,192},{160,224},{192,256},{22... | collective-permute-start | bytes 196616 | tf_op jit(solution)/shard_map/ppermute | solution.py:392
  6.4 5.5 %collective-permute-start = (f32[1,8,2048]{2,1,0:T(8,128)}, f32[1,8,2048]{2,1,0:T(8,128)S(1)}, u32[]{:S(2)}, u32[]{:S(2)}) collective-permute-start(f32[1,8,2048]{2,1,0:T(8,128)} %now.1), channel_id=1, source_target_pairs={{0,32},{32,64},{64,96},{96,128},{128,160},{160,192},{192,224},{224... | collective-permute-start | bytes 196616 | tf_op jit(solution)/shard_map/ppermute | solution.py:393
  9.9 0.9 %copy-start = (f32[3,8,2048]{2,1,0:T(8,128)S(1)}, f32[3,8,2048]{2,1,0:T(8,128)}, u32[]{:S(2)}) copy-start(f32[3,8,2048]{2,1,0:T(8,128)} %terms.1) | copy-start | bytes 589828
  10.8 0.8 %copy-start.1 = (f32[1,8,2048]{2,1,0:T(8,128)S(1)}, f32[1,8,2048]{2,1,0:T(8,128)}, u32[]{:S(2)}) copy-start(f32[1,8,2048]{2,1,0:T(8,128)} %now.1) | copy-start | bytes 196612
  12.1 18.9 %copy-start.2 = (f32[4]{0:T(128)S(1)}, f32[4]{0:T(128)}, u32[]{:S(2)}) copy-start(f32[4]{0:T(128)} %polynomial.1) | copy-start | bytes 52

commit v7 on v6

--- a/solution.py
+++ b/solution.py
@@ -22,6 +22,14 @@
 PARAMS = pltpu.CompilerParams(vmem_limit_bytes=40 * 1024 * 1024)
 
 
+def first_of(strips):
+    return strips // 2 + strips // 8
+
+
+def place(device, strips):
+    return (device - first_of(strips)) % (2 * strips)
+
+
 def tiles_of(source):
     return [source[:, k * LANES : (k + 1) * LANES] for k in range(source.shape[1] // LANES)]
 
@@ -60,7 +68,8 @@
     parts = riders(tiles_of(terms.at[2 * core]), lane)
     across = windows(tiles_of(terms.at[1]), lane)
     upper = (lane >= 0) & (core == 0)
-    for peer, (field, part, drift) in enumerate(zip(fields, parts, across)):
+    for device, (field, part, drift) in enumerate(zip(fields, parts, across)):
+        peer = place(device, out.shape[0] // 2)
         put(out, peer, 0, jnp.where(lane < WIDE, field, part[0]))
         put(out, peer, 1, part[1])
         put(out, peer, 2, part[2])
@@ -74,7 +83,8 @@
         for half in (0, 1, 6):
             out[peer, half] = own[peer, half]
     for plane, source in ((1, before), (2, earlier)):
-        for peer, window in enumerate(windows(tiles_of(source.at[0]), lane)):
+        for device, window in enumerate(windows(tiles_of(source.at[0]), lane)):
+            peer = place(device, out.shape[0] // 2)
             out[peer, 2 * plane] = jnp.where(narrow, window[:HALF], own[peer, 2 * plane])
             out[peer, 2 * plane + 1] = jnp.where(narrow, window[HALF:], own[peer, 2 * plane + 1])
 
@@ -141,7 +151,7 @@
 
     for s in range(strips):
         for c in range(2):
-            peer = c * strips + s
+            peer = place(c * strips + s, strips)
             at = PAD + s * ROWS
             for plane in range(3):
                 k0[times - 2 + c - 2 * plane, at : at + HALF] = got[peer, 2 * plane]
@@ -253,7 +263,7 @@
 
     for c in range(2):
         for s in range(strips):
-            peer = c * strips + s
+            peer = place(c * strips + s, strips)
             at = slice(PAD + s * ROWS, PAD + (s + 1) * ROWS)
             for pair in range(2):
                 low = lifted[2 * pair]
@@ -374,7 +384,8 @@
     low = jnp.where(mine, weights[0], weights[1])
     high = jnp.where(mine, weights[2], weights[3])
 
-    def block(index, part):
+    def block(device, part):
+        index = place(device, got.shape[0] // 2)
         value = low * got[index, part] + high * got[index, 2 + part]
         return pltpu.roll(value, LANES - HALO, 1) + pltpu.roll(value, OWN - HALO, 1)
 
@@ -388,7 +399,11 @@
     f32 = jnp.float32
     peers = 2 * strips
     rows = ROWS * strips
-    layer = ("c", "s")
+    circle = [(first_of(strips) + i) % peers for i in range(peers)]
+
+    def exchange(value):
+        return lax.all_to_all(value, ("c", "s"), 0, 0, axis_index_groups=[circle], tiled=True)
+
     earlier = lax.ppermute(right_side, "z", [(i, i + 2) for i in range(layers - 2)])
     before = lax.ppermute(right_side, "z", [(i, i + 1) for i in range(layers - 1)])
     own = pl.pallas_call(
@@ -408,7 +423,7 @@
         compiler_params=PARAMS,
         name="pack",
     )(own, before, earlier)
-    got = lax.all_to_all(sent, layer, 0, 0, tiled=True)
+    got = exchange(sent)
     times = KRYLOV + 2
     field = lambda count: pltpu.VMEM((count, rows + 2 * PAD, LANES), f32)
     sent = pl.pallas_call(
@@ -423,7 +438,7 @@
         compiler_params=PARAMS,
         name="krylov",
     )(polynomial, got)
-    got = lax.all_to_all(sent, layer, 0, 0, tiled=True)
+    got = exchange(sent)
     partial = jnp.concatenate(exact_sum(got[:, 4, 0, :], got[:, 4, 1, :], 0))
     partial = jnp.broadcast_to(partial[None], (layers, 2, LANES))
     order = [(layers // 2 + i) % layers for i in range(layers)]

time: 68.1 us -> 64.9 us (0.953)
  blocking collectives: 50.7 us -> 47.4 us
    all_to_all x2, blocking collectives: 32.1 us -> 28.9 us  [exchange(): lax.all_to_all(value, ('c', 's'), 0, 0, axis_index_groups=[circle], tiled...]
where the time goes in v7:
time: 64.9 us; the launch traced here: 64.6 us
  blocking collectives  47.4 us (73%)
  starting transfers between devices  9.27 us (14%)
  Pallas kernels  5.29 us (8%)
  local copies, waits for them, and re-layouts  1.8 us (3%)
  between operations  0.71 us (1%)
    all_to_all x2, blocking collectives, exchange(): lax.all_to_all(value, ('c', 's'), 0, 0, axis_index_groups=[circle], tiled...  28.9 us
    all_to_all x1, blocking collectives, body(): lax.all_to_all(partial, 'z', 0, 0, axis_index_groups=[order], tiled=True)  18.5 us
    ppermute x1, starting transfers between devices, body(): lax.ppermute(right_side, 'z', [(i, i + 2) for i in range(layers - 2)])  5.73 us
    pallas_call x1, Pallas kernels, body(): pl.pallas_call(functools.partial(krylov_kernel, strips), out_shape=jax.Sh...  3.72 us
    ppermute x1, starting transfers between devices, body(): lax.ppermute(right_side, 'z', [(i, i + 1) for i in range(layers - 1)])  3.54 us
    unnamed x6, local copies, waits for them, and re-layouts  1.77 us
  transfers between devices with their start and end apart: 2, of which 0 were waited for; matrix products, arithmetic and copies ran while one was open for 0% of the time, Pallas kernels for 0%

profile of v7, /device:TPU:1, one launch (start us, length us, event | category | flops | bytes accessed | tf_op | source)
XLA Modules:
  0.0 64.6 jit_solution(5424626835606685964)
XLA Ops:
  0.6 5.7 %collective-permute-start.1 = (f32[1,8,2048]{2,1,0:T(8,128)}, f32[1,8,2048]{2,1,0:T(8,128)S(1)}, u32[]{:S(2)}, u32[]{:S(2)}) collective-permute-start(f32[1,8,2048]{2,1,0:T(8,128)} %now.1), channel_id=1, source_target_pairs={{0,64},{32,96},{64,128},{96,160},{128,192},{160,224},{192,256},{22... | collective-permute-start | bytes 196616 | tf_op jit(solution)/shard_map/ppermute | solution.py:407
  6.4 3.5 %collective-permute-start = (f32[1,8,2048]{2,1,0:T(8,128)}, f32[1,8,2048]{2,1,0:T(8,128)S(1)}, u32[]{:S(2)}, u32[]{:S(2)}) collective-permute-start(f32[1,8,2048]{2,1,0:T(8,128)} %now.1), channel_id=1, source_target_pairs={{0,32},{32,64},{64,96},{96,128},{128,160},{160,192},{192,224},{224... | collective-permute-start | bytes 196616 | tf_op jit(solution)/shard_map/ppermute | solution.py:408
  9.9 0.0 copy-start
  9.9 0.9 %copy-done = f32[3,8,2048]{2,1,0:T(8,128)S(1)} copy-done((f32[3,8,2048]{2,1,0:T(8,128)S(1)}, f32[3,8,2048]{2,1,0:T(8,128)}, u32[]{:S(2)}) %copy-start) | copy-done | bytes 196632
  10.8 0.0 copy-start.1
  10.8 0.8 %copy-done.1 = f32[1,8,2048]{2,1,0:T(8,128)S(1)} copy-done((f32[1,8,2048]{2,1,0:T(8,128)S(1)}, f32[1,8,2048]{2,1,0:T(8,128)}, u32[]{:S(2)}) %copy-start.1) | copy-done | bytes 65560
  11.7 0.2 own.1
  11.9 0.0 collective-permute-done.1.earlier
  11.9 0.0 collective-permute-done.before
  11.9 0.1 pack.1
  12.1 0.0 copy-start.2
  12.1 16.3 %all_to_all.15.got = f32[32,7,4,128]{3,2,1,0:T(4,128)S(1)} all-to-all(f32[32,7,4,128]{3,2,1,0:T(4,128)S(1)} %pack.1), channel_id=1, replica_groups={{10,11,12,13,14,15,16,17,18,19,20,21,22,23,24,25,26,27,28,29,30,31,0,1,..., dimensions={0} | all-to-all | bytes 917504 | tf_op jit(solution)/shard_map/all_to_all | solution.py:405
  28.3 0.0 copy-done.2
  28.3 3.7 %krylov.1 = f32[32,5,4,128]{3,2,1,0:T(4,128)S(1)} custom-call(f32[4]{0:T(128)S(1)} %copy-done.2, f32[32,7,4,128]{3,2,1,0:T(4,128)S(1)} %all_to_all.15.got), custom_call_target="tpu_custom_call" | custom-call | tf_op jit(solution)/shard_map/krylov/pallas_call | solution.py:429
  32.1 12.6 %all_to_all.16.got = f32[32,5,4,128]{3,2,1,0:T(4,128)S(1)} all-to-all(f32[32,5,4,128]{3,2,1,0:T(4,128)S(1)} %krylov.1), channel_id=1, replica_groups={{10,11,12,13,14,15,16,17,18,19,20,21,22,23,24,25,26,27,28,29,30,31,0,1,..., dimensions={0} | all-to-all | bytes 655360 | tf_op jit(solution)/shard_map/all_to_all | solution.py:405
  44.8 18.5 %all_to_all.17.partial = f32[16,2,128]{2,1,0:T(2,128)S(1)} all-to-all(f32[16,2,128]{2,1,0:T(2,128)S(1)} %broadcast_in_dim.15), channel_id=1, replica_groups={{256,288,320,352,384,416,448,480,0,32,64,96,128,160,192,224},{257,289,3..., dimensions={0} | all-to-all | bytes 32768 | tf_op jit(solution)/shard_map/all_to_all | solution.py:445
  63.3 1.2 %combine.1 = (f32[1,8,2048]{2,1,0:T(8,128)}, f32[4]{0:T(128)}) custom-call(f32[16,2,128]{2,1,0:T(2,128)S(1)} %all_to_all.17.partial, f32[32,5,4,128]{3,2,1,0:T(4,128)S(1)} %all_to_all.16.got), custom_call_target="tpu_custom_call" | custom-call | tf_op jit(solution)/shard_map/combine/pallas_call | solution.py:446
  (6 shorter events, 0.1 us)
Async XLA Ops:
  0.6 11.3 %collective-permute-start.1 = (f32[1,8,2048]{2,1,0:T(8,128)}, f32[1,8,2048]{2,1,0:T(8,128)S(1)}, u32[]{:S(2)}, u32[]{:S(2)}) collective-permute-start(f32[1,8,2048]{2,1,0:T(8,128)} %now.1), channel_id=1, source_target_pairs={{0,64},{32,96},{64,128},{96,160},{128,192},{160,224},{192,256},{22... | collective-permute-start | bytes 196616 | tf_op jit(solution)/shard_map/ppermute | solution.py:407
  6.4 5.5 %collective-permute-start = (f32[1,8,2048]{2,1,0:T(8,128)}, f32[1,8,2048]{2,1,0:T(8,128)S(1)}, u32[]{:S(2)}, u32[]{:S(2)}) collective-permute-start(f32[1,8,2048]{2,1,0:T(8,128)} %now.1), channel_id=1, source_target_pairs={{0,32},{32,64},{64,96},{96,128},{128,160},{160,192},{192,224},{224... | collective-permute-start | bytes 196616 | tf_op jit(solution)/shard_map/ppermute | solution.py:408
  9.9 0.9 %copy-start = (f32[3,8,2048]{2,1,0:T(8,128)S(1)}, f32[3,8,2048]{2,1,0:T(8,128)}, u32[]{:S(2)}) copy-start(f32[3,8,2048]{2,1,0:T(8,128)} %terms.1) | copy-start | bytes 589828
  10.8 0.8 %copy-start.1 = (f32[1,8,2048]{2,1,0:T(8,128)S(1)}, f32[1,8,2048]{2,1,0:T(8,128)}, u32[]{:S(2)}) copy-start(f32[1,8,2048]{2,1,0:T(8,128)} %now.1) | copy-start | bytes 196612
  12.1 16.3 %copy-start.2 = (f32[4]{0:T(128)S(1)}, f32[4]{0:T(128)}, u32[]{:S(2)}) copy-start(f32[4]{0:T(128)} %polynomial.1) | copy-start | bytes 52

commit v8 on v7

--- a/solution.py
+++ b/solution.py
@@ -441,7 +441,7 @@
     got = exchange(sent)
     partial = jnp.concatenate(exact_sum(got[:, 4, 0, :], got[:, 4, 1, :], 0))
     partial = jnp.broadcast_to(partial[None], (layers, 2, LANES))
-    order = [(layers // 2 + i) % layers for i in range(layers)]
+    order = sorted(range(layers), key=lambda i: (i != layers // 2, min(i, layers - i), i))
     partial = lax.all_to_all(partial, "z", 0, 0, axis_index_groups=[order], tiled=True)
     return pl.pallas_call(
         combine_kernel,

time: 64.9 us -> 64.9 us (level)
  no operation moved by 1% of the time
where the time goes in v8:
time: 64.9 us; the launch traced here: 64.3 us
  blocking collectives  47.2 us (73%)
  starting transfers between devices  9.27 us (14%)
  Pallas kernels  5.29 us (8%)
  local copies, waits for them, and re-layouts  1.8 us (3%)
  between operations  0.71 us (1%)
    all_to_all x2, blocking collectives, exchange(): lax.all_to_all(value, ('c', 's'), 0, 0, axis_index_groups=[circle], tiled...  28.9 us
    all_to_all x1, blocking collectives, body(): lax.all_to_all(partial, 'z', 0, 0, axis_index_groups=[order], tiled=True)  18.3 us
    ppermute x1, starting transfers between devices, body(): lax.ppermute(right_side, 'z', [(i, i + 2) for i in range(layers - 2)])  5.73 us
    pallas_call x1, Pallas kernels, body(): pl.pallas_call(functools.partial(krylov_kernel, strips), out_shape=jax.Sh...  3.72 us
    ppermute x1, starting transfers between devices, body(): lax.ppermute(right_side, 'z', [(i, i + 1) for i in range(layers - 1)])  3.54 us
    unnamed x6, local copies, waits for them, and re-layouts  1.77 us
  transfers between devices with their start and end apart: 2, of which 0 were waited for; matrix products, arithmetic and copies ran while one was open for 0% of the time, Pallas kernels for 0%

profile of v8, /device:TPU:1, one launch (start us, length us, event | category | flops | bytes accessed | tf_op | source)
XLA Modules:
  0.0 64.3 jit_solution(10170206738374023950)
XLA Ops:
  0.6 5.7 %collective-permute-start.1 = (f32[1,8,2048]{2,1,0:T(8,128)}, f32[1,8,2048]{2,1,0:T(8,128)S(1)}, u32[]{:S(2)}, u32[]{:S(2)}) collective-permute-start(f32[1,8,2048]{2,1,0:T(8,128)} %now.1), channel_id=1, source_target_pairs={{0,64},{32,96},{64,128},{96,160},{128,192},{160,224},{192,256},{22... | collective-permute-start | bytes 196616 | tf_op jit(solution)/shard_map/ppermute | solution.py:407
  6.4 3.5 %collective-permute-start = (f32[1,8,2048]{2,1,0:T(8,128)}, f32[1,8,2048]{2,1,0:T(8,128)S(1)}, u32[]{:S(2)}, u32[]{:S(2)}) collective-permute-start(f32[1,8,2048]{2,1,0:T(8,128)} %now.1), channel_id=1, source_target_pairs={{0,32},{32,64},{64,96},{96,128},{128,160},{160,192},{192,224},{224... | collective-permute-start | bytes 196616 | tf_op jit(solution)/shard_map/ppermute | solution.py:408
  9.9 0.0 copy-start
  9.9 0.9 %copy-done = f32[3,8,2048]{2,1,0:T(8,128)S(1)} copy-done((f32[3,8,2048]{2,1,0:T(8,128)S(1)}, f32[3,8,2048]{2,1,0:T(8,128)}, u32[]{:S(2)}) %copy-start) | copy-done | bytes 196632
  10.8 0.0 copy-start.1
  10.8 0.8 %copy-done.1 = f32[1,8,2048]{2,1,0:T(8,128)S(1)} copy-done((f32[1,8,2048]{2,1,0:T(8,128)S(1)}, f32[1,8,2048]{2,1,0:T(8,128)}, u32[]{:S(2)}) %copy-start.1) | copy-done | bytes 65560
  11.7 0.2 own.1
  11.9 0.0 collective-permute-done.1.earlier
  11.9 0.0 collective-permute-done.before
  11.9 0.1 pack.1
  12.1 0.0 copy-start.2
  12.1 16.3 %all_to_all.15.got = f32[32,7,4,128]{3,2,1,0:T(4,128)S(1)} all-to-all(f32[32,7,4,128]{3,2,1,0:T(4,128)S(1)} %pack.1), channel_id=1, replica_groups={{10,11,12,13,14,15,16,17,18,19,20,21,22,23,24,25,26,27,28,29,30,31,0,1,..., dimensions={0} | all-to-all | bytes 917504 | tf_op jit(solution)/shard_map/all_to_all | solution.py:405
  28.3 0.0 copy-done.2
  28.3 3.7 %krylov.1 = f32[32,5,4,128]{3,2,1,0:T(4,128)S(1)} custom-call(f32[4]{0:T(128)S(1)} %copy-done.2, f32[32,7,4,128]{3,2,1,0:T(4,128)S(1)} %all_to_all.15.got), custom_call_target="tpu_custom_call" | custom-call | tf_op jit(solution)/shard_map/krylov/pallas_call | solution.py:429
  32.1 12.6 %all_to_all.16.got = f32[32,5,4,128]{3,2,1,0:T(4,128)S(1)} all-to-all(f32[32,5,4,128]{3,2,1,0:T(4,128)S(1)} %krylov.1), channel_id=1, replica_groups={{10,11,12,13,14,15,16,17,18,19,20,21,22,23,24,25,26,27,28,29,30,31,0,1,..., dimensions={0} | all-to-all | bytes 655360 | tf_op jit(solution)/shard_map/all_to_all | solution.py:405
  44.8 18.3 %all_to_all.17.partial = f32[16,2,128]{2,1,0:T(2,128)S(1)} all-to-all(f32[16,2,128]{2,1,0:T(2,128)S(1)} %broadcast_in_dim.15), channel_id=1, replica_groups={{256,0,32,480,64,448,96,416,128,384,160,352,192,320,224,288},{257,1,33,..., dimensions={0} | all-to-all | bytes 32768 | tf_op jit(solution)/shard_map/all_to_all | solution.py:445
  63.1 1.2 %combine.1 = (f32[1,8,2048]{2,1,0:T(8,128)}, f32[4]{0:T(128)}) custom-call(f32[16,2,128]{2,1,0:T(2,128)S(1)} %all_to_all.17.partial, f32[32,5,4,128]{3,2,1,0:T(4,128)S(1)} %all_to_all.16.got), custom_call_target="tpu_custom_call" | custom-call | tf_op jit(solution)/shard_map/combine/pallas_call | solution.py:446
  (6 shorter events, 0.1 us)
Async XLA Ops:
  0.6 11.3 %collective-permute-start.1 = (f32[1,8,2048]{2,1,0:T(8,128)}, f32[1,8,2048]{2,1,0:T(8,128)S(1)}, u32[]{:S(2)}, u32[]{:S(2)}) collective-permute-start(f32[1,8,2048]{2,1,0:T(8,128)} %now.1), channel_id=1, source_target_pairs={{0,64},{32,96},{64,128},{96,160},{128,192},{160,224},{192,256},{22... | collective-permute-start | bytes 196616 | tf_op jit(solution)/shard_map/ppermute | solution.py:407
  6.4 5.5 %collective-permute-start = (f32[1,8,2048]{2,1,0:T(8,128)}, f32[1,8,2048]{2,1,0:T(8,128)S(1)}, u32[]{:S(2)}, u32[]{:S(2)}) collective-permute-start(f32[1,8,2048]{2,1,0:T(8,128)} %now.1), channel_id=1, source_target_pairs={{0,32},{32,64},{64,96},{96,128},{128,160},{160,192},{192,224},{224... | collective-permute-start | bytes 196616 | tf_op jit(solution)/shard_map/ppermute | solution.py:408
  9.9 0.9 %copy-start = (f32[3,8,2048]{2,1,0:T(8,128)S(1)}, f32[3,8,2048]{2,1,0:T(8,128)}, u32[]{:S(2)}) copy-start(f32[3,8,2048]{2,1,0:T(8,128)} %terms.1) | copy-start | bytes 589828
  10.8 0.8 %copy-start.1 = (f32[1,8,2048]{2,1,0:T(8,128)S(1)}, f32[1,8,2048]{2,1,0:T(8,128)}, u32[]{:S(2)}) copy-start(f32[1,8,2048]{2,1,0:T(8,128)} %now.1) | copy-start | bytes 196612
  12.1 16.3 %copy-start.2 = (f32[4]{0:T(128)S(1)}, f32[4]{0:T(128)}, u32[]{:S(2)}) copy-start(f32[4]{0:T(128)} %polynomial.1) | copy-start | bytes 52

commit v9 on v8

--- a/solution.py
+++ b/solution.py
@@ -12,6 +12,7 @@
 HALO = 16
 WIDE = OWN + 2 * HALO
 HALF = 4
+FINE = 2
 LANES = 128
 ROWS = 8
 PAD = 8
@@ -259,7 +260,7 @@
         for kind in range(2):
             packed[kind] = jnp.where(lane == sub + n * ROWS, parts[kind], packed[kind])
     packed = [jnp.sum(value, axis=0, keepdims=True) for value in packed]
-    packed = jnp.where(sub[:HALF] == 0, packed[0], jnp.where(sub[:HALF] == 1, packed[1], 0.0))
+    packed = jnp.where(sub[:FINE] == 0, packed[0], packed[1])
 
     for c in range(2):
         for s in range(strips):
@@ -269,8 +270,10 @@
                 low = lifted[2 * pair]
                 high = lifted[2 * pair + 1]
                 turned = pltpu.roll(high[high.shape[0] - 2 + c, at], OWN, 1)
-                put(out, peer, pair, jnp.where(mine, low[low.shape[0] - 2 + c, at], turned))
-            out[peer, 4] = packed
+                value = jnp.where(mine, low[low.shape[0] - 2 + c, at], turned)
+                for part in range(ROWS // FINE):
+                    out[peer, 4 * pair + part] = value[part * FINE : (part + 1) * FINE]
+            out[peer, 8] = packed
 
 
 def least_squares(columns, beta_norm):
@@ -379,20 +382,20 @@
     weights, norms = cycle(gram)
     for n, norm in enumerate(norms):
         history[n] = jnp.max(norm)
-    half = lane[:HALF]
+    half = lane[:FINE]
     mine = (half >= HALO) & (half < HALO + OWN)
     low = jnp.where(mine, weights[0], weights[1])
     high = jnp.where(mine, weights[2], weights[3])
 
     def block(device, part):
         index = place(device, got.shape[0] // 2)
-        value = low * got[index, part] + high * got[index, 2 + part]
+        value = low * got[index, part] + high * got[index, 4 + part]
         return pltpu.roll(value, LANES - HALO, 1) + pltpu.roll(value, OWN - HALO, 1)
 
     for k in range(got.shape[0] // 2):
-        for part in range(2):
+        for part in range(ROWS // FINE):
             value = jnp.where(half < OWN, block(2 * k, part), block(2 * k + 1, part))
-            solution[0, part * HALF : (part + 1) * HALF, k * LANES : (k + 1) * LANES] = value
+            solution[0, part * FINE : (part + 1) * FINE, k * LANES : (k + 1) * LANES] = value
 
 
 def body(layers, strips, right_side, cell_terms, polynomial):
@@ -428,7 +431,7 @@
     field = lambda count: pltpu.VMEM((count, rows + 2 * PAD, LANES), f32)
     sent = pl.pallas_call(
         functools.partial(krylov_kernel, strips),
-        out_shape=jax.ShapeDtypeStruct((peers, 5, HALF, LANES), f32),
+        out_shape=jax.ShapeDtypeStruct((peers, 9, FINE, LANES), f32),
         in_specs=[SMEM, VMEM],
         out_specs=VMEM,
         scratch_shapes=[pltpu.VMEM((5, rows, LANES), f32)] * 2
@@ -439,7 +442,7 @@
         name="krylov",
     )(polynomial, got)
     got = exchange(sent)
-    partial = jnp.concatenate(exact_sum(got[:, 4, 0, :], got[:, 4, 1, :], 0))
+    partial = jnp.concatenate(exact_sum(got[:, 8, 0, :], got[:, 8, 1, :], 0))
     partial = jnp.broadcast_to(partial[None], (layers, 2, LANES))
     order = sorted(range(layers), key=lambda i: (i != layers // 2, min(i, layers - i), i))
     partial = lax.all_to_all(partial, "z", 0, 0, axis_index_groups=[order], tiled=True)

time: 64.9 us -> 64.7 us (level)
  no operation moved by 1% of the time
where the time goes in v9:
time: 64.7 us; the launch traced here: 64.1 us
  blocking collectives  46.8 us (72%)
  starting transfers between devices  9.27 us (14%)
  Pallas kernels  5.43 us (8%)
  local copies, waits for them, and re-layouts  1.8 us (3%)
  between operations  0.71 us (1%)
    all_to_all x2, blocking collectives, exchange(): lax.all_to_all(value, ('c', 's'), 0, 0, axis_index_groups=[circle], tiled...  28.5 us
    all_to_all x1, blocking collectives, body(): lax.all_to_all(partial, 'z', 0, 0, axis_index_groups=[order], tiled=True)  18.3 us
    ppermute x1, starting transfers between devices, body(): lax.ppermute(right_side, 'z', [(i, i + 2) for i in range(layers - 2)])  5.73 us
    pallas_call x1, Pallas kernels, body(): pl.pallas_call(functools.partial(krylov_kernel, strips), out_shape=jax.Sh...  3.72 us
    ppermute x1, starting transfers between devices, body(): lax.ppermute(right_side, 'z', [(i, i + 1) for i in range(layers - 1)])  3.54 us
    unnamed x6, local copies, waits for them, and re-layouts  1.77 us
    pallas_call x1, Pallas kernels, body(): pl.pallas_call(combine_kernel, out_shape=(jax.ShapeDtypeStruct(right_side...  1.38 us
  transfers between devices with their start and end apart: 2, of which 0 were waited for; matrix products, arithmetic and copies ran while one was open for 0% of the time, Pallas kernels for 0%

profile of v9, /device:TPU:1, one launch (start us, length us, event | category | flops | bytes accessed | tf_op | source)
XLA Modules:
  0.0 64.1 jit_solution(17865523971468380371)
XLA Ops:
  0.6 5.7 %collective-permute-start.1 = (f32[1,8,2048]{2,1,0:T(8,128)}, f32[1,8,2048]{2,1,0:T(8,128)S(1)}, u32[]{:S(2)}, u32[]{:S(2)}) collective-permute-start(f32[1,8,2048]{2,1,0:T(8,128)} %now.1), channel_id=1, source_target_pairs={{0,64},{32,96},{64,128},{96,160},{128,192},{160,224},{192,256},{22... | collective-permute-start | bytes 196616 | tf_op jit(solution)/shard_map/ppermute | solution.py:410
  6.4 3.5 %collective-permute-start = (f32[1,8,2048]{2,1,0:T(8,128)}, f32[1,8,2048]{2,1,0:T(8,128)S(1)}, u32[]{:S(2)}, u32[]{:S(2)}) collective-permute-start(f32[1,8,2048]{2,1,0:T(8,128)} %now.1), channel_id=1, source_target_pairs={{0,32},{32,64},{64,96},{96,128},{128,160},{160,192},{192,224},{224... | collective-permute-start | bytes 196616 | tf_op jit(solution)/shard_map/ppermute | solution.py:411
  9.9 0.0 copy-start
  9.9 0.9 %copy-done = f32[3,8,2048]{2,1,0:T(8,128)S(1)} copy-done((f32[3,8,2048]{2,1,0:T(8,128)S(1)}, f32[3,8,2048]{2,1,0:T(8,128)}, u32[]{:S(2)}) %copy-start) | copy-done | bytes 196632
  10.8 0.0 copy-start.1
  10.8 0.8 %copy-done.1 = f32[1,8,2048]{2,1,0:T(8,128)S(1)} copy-done((f32[1,8,2048]{2,1,0:T(8,128)S(1)}, f32[1,8,2048]{2,1,0:T(8,128)}, u32[]{:S(2)}) %copy-start.1) | copy-done | bytes 65560
  11.7 0.2 own.1
  11.9 0.0 collective-permute-done.1.earlier
  11.9 0.0 collective-permute-done.before
  11.9 0.1 pack.1
  12.1 0.0 copy-start.2
  12.1 16.3 %all_to_all.15.got = f32[32,7,4,128]{3,2,1,0:T(4,128)S(1)} all-to-all(f32[32,7,4,128]{3,2,1,0:T(4,128)S(1)} %pack.1), channel_id=1, replica_groups={{10,11,12,13,14,15,16,17,18,19,20,21,22,23,24,25,26,27,28,29,30,31,0,1,..., dimensions={0} | all-to-all | bytes 917504 | tf_op jit(solution)/shard_map/all_to_all | solution.py:408
  28.3 0.0 copy-done.2
  28.3 3.7 %krylov.1 = f32[32,9,2,128]{3,2,1,0:T(2,128)S(1)} custom-call(f32[4]{0:T(128)S(1)} %copy-done.2, f32[32,7,4,128]{3,2,1,0:T(4,128)S(1)} %all_to_all.15.got), custom_call_target="tpu_custom_call" | custom-call | tf_op jit(solution)/shard_map/krylov/pallas_call | solution.py:432
  32.1 12.3 %all_to_all.16.got = f32[32,9,2,128]{3,2,1,0:T(2,128)S(1)} all-to-all(f32[32,9,2,128]{3,2,1,0:T(2,128)S(1)} %krylov.1), channel_id=1, replica_groups={{10,11,12,13,14,15,16,17,18,19,20,21,22,23,24,25,26,27,28,29,30,31,0,1,..., dimensions={0} | all-to-all | bytes 589824 | tf_op jit(solution)/shard_map/all_to_all | solution.py:408
  44.4 18.3 %all_to_all.17.partial = f32[16,2,128]{2,1,0:T(2,128)S(1)} all-to-all(f32[16,2,128]{2,1,0:T(2,128)S(1)} %broadcast_in_dim.15), channel_id=1, replica_groups={{256,0,32,480,64,448,96,416,128,384,160,352,192,320,224,288},{257,1,33,..., dimensions={0} | all-to-all | bytes 32768 | tf_op jit(solution)/shard_map/all_to_all | solution.py:448
  62.7 1.4 %combine.1 = (f32[1,8,2048]{2,1,0:T(8,128)}, f32[4]{0:T(128)}) custom-call(f32[16,2,128]{2,1,0:T(2,128)S(1)} %all_to_all.17.partial, f32[32,9,2,128]{3,2,1,0:T(2,128)S(1)} %all_to_all.16.got), custom_call_target="tpu_custom_call" | custom-call | tf_op jit(solution)/shard_map/combine/pallas_call | solution.py:449
  (6 shorter events, 0.1 us)
Async XLA Ops:
  0.6 11.3 %collective-permute-start.1 = (f32[1,8,2048]{2,1,0:T(8,128)}, f32[1,8,2048]{2,1,0:T(8,128)S(1)}, u32[]{:S(2)}, u32[]{:S(2)}) collective-permute-start(f32[1,8,2048]{2,1,0:T(8,128)} %now.1), channel_id=1, source_target_pairs={{0,64},{32,96},{64,128},{96,160},{128,192},{160,224},{192,256},{22... | collective-permute-start | bytes 196616 | tf_op jit(solution)/shard_map/ppermute | solution.py:410
  6.4 5.5 %collective-permute-start = (f32[1,8,2048]{2,1,0:T(8,128)}, f32[1,8,2048]{2,1,0:T(8,128)S(1)}, u32[]{:S(2)}, u32[]{:S(2)}) collective-permute-start(f32[1,8,2048]{2,1,0:T(8,128)} %now.1), channel_id=1, source_target_pairs={{0,32},{32,64},{64,96},{96,128},{128,160},{160,192},{192,224},{224... | collective-permute-start | bytes 196616 | tf_op jit(solution)/shard_map/ppermute | solution.py:411
  9.9 0.9 %copy-start = (f32[3,8,2048]{2,1,0:T(8,128)S(1)}, f32[3,8,2048]{2,1,0:T(8,128)}, u32[]{:S(2)}) copy-start(f32[3,8,2048]{2,1,0:T(8,128)} %terms.1) | copy-start | bytes 589828
  10.8 0.8 %copy-start.1 = (f32[1,8,2048]{2,1,0:T(8,128)S(1)}, f32[1,8,2048]{2,1,0:T(8,128)}, u32[]{:S(2)}) copy-start(f32[1,8,2048]{2,1,0:T(8,128)} %now.1) | copy-start | bytes 196612
  12.1 16.3 %copy-start.2 = (f32[4]{0:T(128)S(1)}, f32[4]{0:T(128)}, u32[]{:S(2)}) copy-start(f32[4]{0:T(128)} %polynomial.1) | copy-start | bytes 52

commit v10 on v9

--- a/solution.py
+++ b/solution.py
@@ -444,7 +444,7 @@
     got = exchange(sent)
     partial = jnp.concatenate(exact_sum(got[:, 8, 0, :], got[:, 8, 1, :], 0))
     partial = jnp.broadcast_to(partial[None], (layers, 2, LANES))
-    order = sorted(range(layers), key=lambda i: (i != layers // 2, min(i, layers - i), i))
+    order = sorted(range(layers), key=lambda i: (i != layers // 2 + 1, min(i, layers - i), i))
     partial = lax.all_to_all(partial, "z", 0, 0, axis_index_groups=[order], tiled=True)
     return pl.pallas_call(
         combine_kernel,

time: 64.7 us -> 64.7 us (level)
  no operation moved by 1% of the time
where the time goes in v10:
time: 64.7 us; the launch traced here: 64.1 us
  blocking collectives  46.8 us (72%)
  starting transfers between devices  9.27 us (14%)
  Pallas kernels  5.43 us (8%)
  local copies, waits for them, and re-layouts  1.8 us (3%)
  between operations  0.71 us (1%)
    all_to_all x2, blocking collectives, exchange(): lax.all_to_all(value, ('c', 's'), 0, 0, axis_index_groups=[circle], tiled...  28.5 us
    all_to_all x1, blocking collectives, body(): lax.all_to_all(partial, 'z', 0, 0, axis_index_groups=[order], tiled=True)  18.3 us
    ppermute x1, starting transfers between devices, body(): lax.ppermute(right_side, 'z', [(i, i + 2) for i in range(layers - 2)])  5.73 us
    pallas_call x1, Pallas kernels, body(): pl.pallas_call(functools.partial(krylov_kernel, strips), out_shape=jax.Sh...  3.72 us
    ppermute x1, starting transfers between devices, body(): lax.ppermute(right_side, 'z', [(i, i + 1) for i in range(layers - 1)])  3.54 us
    unnamed x6, local copies, waits for them, and re-layouts  1.77 us
    pallas_call x1, Pallas kernels, body(): pl.pallas_call(combine_kernel, out_shape=(jax.ShapeDtypeStruct(right_side...  1.38 us
  transfers between devices with their start and end apart: 2, of which 0 were waited for; matrix products, arithmetic and copies ran while one was open for 0% of the time, Pallas kernels for 0%

profile of v10, /device:TPU:1, one launch (start us, length us, event | category | flops | bytes accessed | tf_op | source)
XLA Modules:
  0.0 64.1 jit_solution(388312845696616951)
XLA Ops:
  0.6 5.7 %collective-permute-start.1 = (f32[1,8,2048]{2,1,0:T(8,128)}, f32[1,8,2048]{2,1,0:T(8,128)S(1)}, u32[]{:S(2)}, u32[]{:S(2)}) collective-permute-start(f32[1,8,2048]{2,1,0:T(8,128)} %now.1), channel_id=1, source_target_pairs={{0,64},{32,96},{64,128},{96,160},{128,192},{160,224},{192,256},{22... | collective-permute-start | bytes 196616 | tf_op jit(solution)/shard_map/ppermute | solution.py:410
  6.4 3.5 %collective-permute-start = (f32[1,8,2048]{2,1,0:T(8,128)}, f32[1,8,2048]{2,1,0:T(8,128)S(1)}, u32[]{:S(2)}, u32[]{:S(2)}) collective-permute-start(f32[1,8,2048]{2,1,0:T(8,128)} %now.1), channel_id=1, source_target_pairs={{0,32},{32,64},{64,96},{96,128},{128,160},{160,192},{192,224},{224... | collective-permute-start | bytes 196616 | tf_op jit(solution)/shard_map/ppermute | solution.py:411
  9.9 0.0 copy-start
  9.9 0.9 %copy-done = f32[3,8,2048]{2,1,0:T(8,128)S(1)} copy-done((f32[3,8,2048]{2,1,0:T(8,128)S(1)}, f32[3,8,2048]{2,1,0:T(8,128)}, u32[]{:S(2)}) %copy-start) | copy-done | bytes 196632
  10.8 0.0 copy-start.1
  10.8 0.8 %copy-done.1 = f32[1,8,2048]{2,1,0:T(8,128)S(1)} copy-done((f32[1,8,2048]{2,1,0:T(8,128)S(1)}, f32[1,8,2048]{2,1,0:T(8,128)}, u32[]{:S(2)}) %copy-start.1) | copy-done | bytes 65560
  11.7 0.2 own.1
  11.9 0.0 collective-permute-done.1.earlier
  11.9 0.0 collective-permute-done.before
  11.9 0.1 pack.1
  12.1 0.0 copy-start.2
  12.1 16.3 %all_to_all.15.got = f32[32,7,4,128]{3,2,1,0:T(4,128)S(1)} all-to-all(f32[32,7,4,128]{3,2,1,0:T(4,128)S(1)} %pack.1), channel_id=1, replica_groups={{10,11,12,13,14,15,16,17,18,19,20,21,22,23,24,25,26,27,28,29,30,31,0,1,..., dimensions={0} | all-to-all | bytes 917504 | tf_op jit(solution)/shard_map/all_to_all | solution.py:408
  28.3 0.0 copy-done.2
  28.3 3.7 %krylov.1 = f32[32,9,2,128]{3,2,1,0:T(2,128)S(1)} custom-call(f32[4]{0:T(128)S(1)} %copy-done.2, f32[32,7,4,128]{3,2,1,0:T(4,128)S(1)} %all_to_all.15.got), custom_call_target="tpu_custom_call" | custom-call | tf_op jit(solution)/shard_map/krylov/pallas_call | solution.py:432
  32.1 12.3 %all_to_all.16.got = f32[32,9,2,128]{3,2,1,0:T(2,128)S(1)} all-to-all(f32[32,9,2,128]{3,2,1,0:T(2,128)S(1)} %krylov.1), channel_id=1, replica_groups={{10,11,12,13,14,15,16,17,18,19,20,21,22,23,24,25,26,27,28,29,30,31,0,1,..., dimensions={0} | all-to-all | bytes 589824 | tf_op jit(solution)/shard_map/all_to_all | solution.py:408
  44.4 18.3 %all_to_all.17.partial = f32[16,2,128]{2,1,0:T(2,128)S(1)} all-to-all(f32[16,2,128]{2,1,0:T(2,128)S(1)} %broadcast_in_dim.15), channel_id=1, replica_groups={{288,0,32,480,64,448,96,416,128,384,160,352,192,320,224,256},{289,1,33,..., dimensions={0} | all-to-all | bytes 32768 | tf_op jit(solution)/shard_map/all_to_all | solution.py:448
  62.7 1.4 %combine.1 = (f32[1,8,2048]{2,1,0:T(8,128)}, f32[4]{0:T(128)}) custom-call(f32[16,2,128]{2,1,0:T(2,128)S(1)} %all_to_all.17.partial, f32[32,9,2,128]{3,2,1,0:T(2,128)S(1)} %all_to_all.16.got), custom_call_target="tpu_custom_call" | custom-call | tf_op jit(solution)/shard_map/combine/pallas_call | solution.py:449
  (6 shorter events, 0.1 us)
Async XLA Ops:
  0.6 11.3 %collective-permute-start.1 = (f32[1,8,2048]{2,1,0:T(8,128)}, f32[1,8,2048]{2,1,0:T(8,128)S(1)}, u32[]{:S(2)}, u32[]{:S(2)}) collective-permute-start(f32[1,8,2048]{2,1,0:T(8,128)} %now.1), channel_id=1, source_target_pairs={{0,64},{32,96},{64,128},{96,160},{128,192},{160,224},{192,256},{22... | collective-permute-start | bytes 196616 | tf_op jit(solution)/shard_map/ppermute | solution.py:410
  6.4 5.5 %collective-permute-start = (f32[1,8,2048]{2,1,0:T(8,128)}, f32[1,8,2048]{2,1,0:T(8,128)S(1)}, u32[]{:S(2)}, u32[]{:S(2)}) collective-permute-start(f32[1,8,2048]{2,1,0:T(8,128)} %now.1), channel_id=1, source_target_pairs={{0,32},{32,64},{64,96},{96,128},{128,160},{160,192},{192,224},{224... | collective-permute-start | bytes 196616 | tf_op jit(solution)/shard_map/ppermute | solution.py:411
  9.9 0.9 %copy-start = (f32[3,8,2048]{2,1,0:T(8,128)S(1)}, f32[3,8,2048]{2,1,0:T(8,128)}, u32[]{:S(2)}) copy-start(f32[3,8,2048]{2,1,0:T(8,128)} %terms.1) | copy-start | bytes 589828
  10.8 0.8 %copy-start.1 = (f32[1,8,2048]{2,1,0:T(8,128)S(1)}, f32[1,8,2048]{2,1,0:T(8,128)}, u32[]{:S(2)}) copy-start(f32[1,8,2048]{2,1,0:T(8,128)} %now.1) | copy-start | bytes 196612
  12.1 16.3 %copy-start.2 = (f32[4]{0:T(128)S(1)}, f32[4]{0:T(128)}, u32[]{:S(2)}) copy-start(f32[4]{0:T(128)} %polynomial.1) | copy-start | bytes 52

commit v11 on v9

--- a/solution.py
+++ b/solution.py
@@ -24,7 +24,7 @@
 
 
 def first_of(strips):
-    return strips // 2 + strips // 8
+    return strips + strips // 2 + strips // 8
 
 
 def place(device, strips):

time: 64.7 us -> 64.2 us (level)
  no operation moved by 1% of the time
where the time goes in v11:
time: 64.2 us; the launch traced here: 63.6 us
  blocking collectives  46.3 us (72%)
  starting transfers between devices  9.27 us (14%)
  Pallas kernels  5.43 us (8%)
  local copies, waits for them, and re-layouts  1.8 us (3%)
  between operations  0.71 us (1%)
    all_to_all x2, blocking collectives, exchange(): lax.all_to_all(value, ('c', 's'), 0, 0, axis_index_groups=[circle], tiled...  28 us
    all_to_all x1, blocking collectives, body(): lax.all_to_all(partial, 'z', 0, 0, axis_index_groups=[order], tiled=True)  18.3 us
    ppermute x1, starting transfers between devices, body(): lax.ppermute(right_side, 'z', [(i, i + 2) for i in range(layers - 2)])  5.73 us
    pallas_call x1, Pallas kernels, body(): pl.pallas_call(functools.partial(krylov_kernel, strips), out_shape=jax.Sh...  3.72 us
    ppermute x1, starting transfers between devices, body(): lax.ppermute(right_side, 'z', [(i, i + 1) for i in range(layers - 1)])  3.54 us
    unnamed x6, local copies, waits for them, and re-layouts  1.77 us
    pallas_call x1, Pallas kernels, body(): pl.pallas_call(combine_kernel, out_shape=(jax.ShapeDtypeStruct(right_side...  1.38 us
  transfers between devices with their start and end apart: 2, of which 0 were waited for; matrix products, arithmetic and copies ran while one was open for 0% of the time, Pallas kernels for 0%

profile of v11, /device:TPU:1, one launch (start us, length us, event | category | flops | bytes accessed | tf_op | source)
XLA Modules:
  0.0 63.6 jit_solution(1181693205806575791)
XLA Ops:
  0.6 5.7 %collective-permute-start.1 = (f32[1,8,2048]{2,1,0:T(8,128)}, f32[1,8,2048]{2,1,0:T(8,128)S(1)}, u32[]{:S(2)}, u32[]{:S(2)}) collective-permute-start(f32[1,8,2048]{2,1,0:T(8,128)} %now.1), channel_id=1, source_target_pairs={{0,64},{32,96},{64,128},{96,160},{128,192},{160,224},{192,256},{22... | collective-permute-start | bytes 196616 | tf_op jit(solution)/shard_map/ppermute | solution.py:410
  6.4 3.5 %collective-permute-start = (f32[1,8,2048]{2,1,0:T(8,128)}, f32[1,8,2048]{2,1,0:T(8,128)S(1)}, u32[]{:S(2)}, u32[]{:S(2)}) collective-permute-start(f32[1,8,2048]{2,1,0:T(8,128)} %now.1), channel_id=1, source_target_pairs={{0,32},{32,64},{64,96},{96,128},{128,160},{160,192},{192,224},{224... | collective-permute-start | bytes 196616 | tf_op jit(solution)/shard_map/ppermute | solution.py:411
  9.9 0.0 copy-start
  9.9 0.9 %copy-done = f32[3,8,2048]{2,1,0:T(8,128)S(1)} copy-done((f32[3,8,2048]{2,1,0:T(8,128)S(1)}, f32[3,8,2048]{2,1,0:T(8,128)}, u32[]{:S(2)}) %copy-start) | copy-done | bytes 196632
  10.8 0.0 copy-start.1
  10.8 0.8 %copy-done.1 = f32[1,8,2048]{2,1,0:T(8,128)S(1)} copy-done((f32[1,8,2048]{2,1,0:T(8,128)S(1)}, f32[1,8,2048]{2,1,0:T(8,128)}, u32[]{:S(2)}) %copy-start.1) | copy-done | bytes 65560
  11.7 0.2 own.1
  11.9 0.0 collective-permute-done.1.earlier
  11.9 0.0 collective-permute-done.before
  11.9 0.1 pack.1
  12.1 0.0 copy-start.2
  12.1 16.0 %all_to_all.15.got = f32[32,7,4,128]{3,2,1,0:T(4,128)S(1)} all-to-all(f32[32,7,4,128]{3,2,1,0:T(4,128)S(1)} %pack.1), channel_id=1, replica_groups={{26,27,28,29,30,31,0,1,2,3,4,5,6,7,8,9,10,11,12,13,14,15,16,17,18,19,20..., dimensions={0} | all-to-all | bytes 917504 | tf_op jit(solution)/shard_map/all_to_all | solution.py:408
  28.0 0.0 copy-done.2
  28.0 3.7 %krylov.1 = f32[32,9,2,128]{3,2,1,0:T(2,128)S(1)} custom-call(f32[4]{0:T(128)S(1)} %copy-done.2, f32[32,7,4,128]{3,2,1,0:T(4,128)S(1)} %all_to_all.15.got), custom_call_target="tpu_custom_call" | custom-call | tf_op jit(solution)/shard_map/krylov/pallas_call | solution.py:432
  31.7 12.1 %all_to_all.16.got = f32[32,9,2,128]{3,2,1,0:T(2,128)S(1)} all-to-all(f32[32,9,2,128]{3,2,1,0:T(2,128)S(1)} %krylov.1), channel_id=1, replica_groups={{26,27,28,29,30,31,0,1,2,3,4,5,6,7,8,9,10,11,12,13,14,15,16,17,18,19,20..., dimensions={0} | all-to-all | bytes 589824 | tf_op jit(solution)/shard_map/all_to_all | solution.py:408
  43.9 18.3 %all_to_all.17.partial = f32[16,2,128]{2,1,0:T(2,128)S(1)} all-to-all(f32[16,2,128]{2,1,0:T(2,128)S(1)} %broadcast_in_dim.15), channel_id=1, replica_groups={{256,0,32,480,64,448,96,416,128,384,160,352,192,320,224,288},{257,1,33,..., dimensions={0} | all-to-all | bytes 32768 | tf_op jit(solution)/shard_map/all_to_all | solution.py:448
  62.2 1.4 %combine.1 = (f32[1,8,2048]{2,1,0:T(8,128)}, f32[4]{0:T(128)}) custom-call(f32[16,2,128]{2,1,0:T(2,128)S(1)} %all_to_all.17.partial, f32[32,9,2,128]{3,2,1,0:T(2,128)S(1)} %all_to_all.16.got), custom_call_target="tpu_custom_call" | custom-call | tf_op jit(solution)/shard_map/combine/pallas_call | solution.py:449
  (6 shorter events, 0.1 us)
Async XLA Ops:
  0.6 11.3 %collective-permute-start.1 = (f32[1,8,2048]{2,1,0:T(8,128)}, f32[1,8,2048]{2,1,0:T(8,128)S(1)}, u32[]{:S(2)}, u32[]{:S(2)}) collective-permute-start(f32[1,8,2048]{2,1,0:T(8,128)} %now.1), channel_id=1, source_target_pairs={{0,64},{32,96},{64,128},{96,160},{128,192},{160,224},{192,256},{22... | collective-permute-start | bytes 196616 | tf_op jit(solution)/shard_map/ppermute | solution.py:410
  6.4 5.5 %collective-permute-start = (f32[1,8,2048]{2,1,0:T(8,128)}, f32[1,8,2048]{2,1,0:T(8,128)S(1)}, u32[]{:S(2)}, u32[]{:S(2)}) collective-permute-start(f32[1,8,2048]{2,1,0:T(8,128)} %now.1), channel_id=1, source_target_pairs={{0,32},{32,64},{64,96},{96,128},{128,160},{160,192},{192,224},{224... | collective-permute-start | bytes 196616 | tf_op jit(solution)/shard_map/ppermute | solution.py:411
  9.9 0.9 %copy-start = (f32[3,8,2048]{2,1,0:T(8,128)S(1)}, f32[3,8,2048]{2,1,0:T(8,128)}, u32[]{:S(2)}) copy-start(f32[3,8,2048]{2,1,0:T(8,128)} %terms.1) | copy-start | bytes 589828
  10.8 0.8 %copy-start.1 = (f32[1,8,2048]{2,1,0:T(8,128)S(1)}, f32[1,8,2048]{2,1,0:T(8,128)}, u32[]{:S(2)}) copy-start(f32[1,8,2048]{2,1,0:T(8,128)} %now.1) | copy-start | bytes 196612
  12.1 16.0 %copy-start.2 = (f32[4]{0:T(128)S(1)}, f32[4]{0:T(128)}, u32[]{:S(2)}) copy-start(f32[4]{0:T(128)} %polynomial.1) | copy-start | bytes 52
